TPU v7x, 32 devices: a whole 2x2x4 slice. The times are simulated.
32 devices in a mesh: rad: 4 (over y, x), azi: 8 (over z, core).
Axes of the slice: x: 2, y: 2, z: 4, core: 2. Of those that a mesh axis runs over, the one named last changes fastest.
Arguments:
- relative_base_heat: float32 [64, 256, 512], P('rad', 'azi'), may hold values from 0.75 to 1.25
- base_deformation_size: float32 [64, 256, 512], P('rad', 'azi'), may hold values from 0.25 to 1
- base_streamwise_flux: float32 [64, 256, 512], P('rad', 'azi'), may hold values from 0.2 to 1
- goal_heat_change: float32 [64, 256, 512], P('rad', 'azi'), may hold values from 0.25 to 2
- initial_costate_heat: float32 [64, 256, 512], P('rad', 'azi'), may hold values from 0.2 to 2
Outputs:
- temperature_adjoint: float32 [64, 256, 512], P('rad', 'azi')
- lengthwise_velocity_sensitivity: float32 [64, 256, 512], P('rad', 'azi')
All inputs are finite; a program needn't handle non-finite values.
Results may differ from a plain program's by a relative error of at most 0.00045.
Values sent between devices are 32-bit elements; how exact they have to be, the bound alone decides.
A program may use at most 128 MiB of HBM per device.

v0:
```python
import jax
import jax.numpy as jnp
from jax import lax
from jax.sharding import PartitionSpec as P

radial_weight = 8.0
azimuth_weight = 0.25
axial_weight = 0.25
flow_weight = 0.5
mass_weight = 1.0
heat_weight = 0.25
arrhenius_exponent = 2.0
slope_weight = 2.0


def prefix(value, axis, join, neutral, backward):
    count, mine = (lax.axis_size(axis), lax.axis_index(axis))
    pieces = jax.tree.map(lambda part: lax.all_gather(part, axis), value)
    if backward:
        pieces = jax.tree.map(lambda part: part[::-1], pieces)
        mine = count - 1 - mine
    running = jax.tree.map(
        lambda part, zero: jnp.full_like(part, 0) + jnp.asarray(zero, part.dtype), value, neutral
    )

    def lap(position, running):
        longer = join(running, jax.tree.map(lambda part: part[position], pieces))
        return jax.tree.map(lambda new, old: jnp.where(position < mine, new, old), longer, running)

    return lax.fori_loop(0, count - 1, lap, running)


def padded(block, sides, width):
    for axis, dim in sides:
        count = lax.axis_size(axis)
        forward = [(i, i + 1) for i in range(count - 1)]
        forward.append((count - 1, 0))
        backward = [(target, source) for source, target in forward]
        low = lax.ppermute(
            lax.slice_in_dim(block, block.shape[dim] - width, None, axis=dim), axis, forward
        )
        high = lax.ppermute(lax.slice_in_dim(block, 0, width, axis=dim), axis, backward)
        block = jnp.concatenate([low, block, high], axis=dim)
    return block


def line_geometry(first_row, number_lines_total, total_rows, segment_rows):
    row_int = jnp.arange(number_lines_total, dtype=jnp.int32) + first_row
    row_float = row_int.astype(jnp.float32)
    total_float = float(total_rows)
    segment_float = float(segment_rows)
    radius = 1.0 + (row_float + 0.5) / total_float
    inner_face = 1.0 + row_float / total_float
    outer_face = 1.0 + (row_float + 1.0) / total_float
    stiffness = radial_weight * segment_float * segment_float
    lower_off = jnp.where(row_int == 0, 0.0, -stiffness * inner_face / radius)
    upper_off = jnp.where(row_int == total_rows - 1, 0.0, -stiffness * outer_face / radius)
    radial_diag = stiffness * (inner_face + outer_face) / radius
    azimuth_coef = azimuth_weight / (radius * radius)
    return (lower_off, upper_off, radial_diag, azimuth_coef)


def plate_arrays(relative_base_heat, base_deformation_size, base_streamwise_flux):
    polymer_resistance = jnp.exp(-arrhenius_exponent * (relative_base_heat - 1.0))
    heating = (
        heat_weight
        * arrhenius_exponent
        * polymer_resistance
        * base_deformation_size
        * base_deformation_size
    )
    transport_factor = flow_weight * base_streamwise_flux
    extra_pivot_entry = mass_weight + 2.0 * axial_weight + transport_factor + heating
    return (polymer_resistance, transport_factor, extra_pivot_entry)


def explicit_rhs(old_center, side_sum, azimuth_coef, transport_factor, source_field):
    edge_nulls = jnp.zeros_like(old_center[:, :, :1])
    next_cell = jnp.concatenate([old_center[:, :, 1:], edge_nulls], axis=2)
    prev_cell = jnp.concatenate([edge_nulls, old_center[:, :, :-1]], axis=2)
    return (
        source_field
        + azimuth_coef[:, None, None] * side_sum
        + axial_weight * (prev_cell + next_cell)
        + transport_factor * next_cell
        + mass_weight * old_center
    )


def velocity_factor(relative_base_heat, polymer_resistance, base_deformation_size):
    edge_nulls = jnp.zeros_like(relative_base_heat[:, :, :1])
    resistance_derivative_array = jnp.concatenate(
        [relative_base_heat[:, :, 1:] - relative_base_heat[:, :, :-1], edge_nulls], axis=2
    )
    return (
        slope_weight * resistance_derivative_array
        - 2.0 * heat_weight * polymer_resistance * base_deformation_size
    )


def compose_maps(earlier, later):
    first_entry = later[0] * earlier[0]
    second_entry = later[0] * earlier[1] + later[1] * earlier[3] + later[2] * earlier[5]
    third_entry = later[0] * earlier[2] + later[1] * earlier[4] + later[2]
    fourth_entry = later[3] * earlier[3] + later[4] * earlier[5]
    fifth_entry = later[3] * earlier[4] + later[4]
    sixth_entry = later[5] * earlier[3] + earlier[5]
    inverse_norm = 1.0 / (later[5] * earlier[4] + 1.0)
    return (
        first_entry * inverse_norm,
        second_entry * inverse_norm,
        third_entry * inverse_norm,
        fourth_entry * inverse_norm,
        fifth_entry * inverse_norm,
        sixth_entry * inverse_norm,
    )


def compose_affine(earlier, later):
    return (later[0] + later[1] * earlier[0], later[1] * earlier[1])


def solve_lines(lower_off, diagonal, upper_off, right_side):
    number_lines_total = right_side.shape[0]
    zero_plane = jnp.zeros_like(right_side[0])
    unit_plane = jnp.ones_like(right_side[0])
    unit_map = (unit_plane, zero_plane, zero_plane, unit_plane, zero_plane, zero_plane)
    transfer = unit_map
    for index_of_row in range(number_lines_total):
        inverse_diag = 1.0 / diagonal[index_of_row]
        pivot_ratio = -lower_off[index_of_row] * inverse_diag
        step_map = (
            pivot_ratio,
            zero_plane,
            right_side[index_of_row] * inverse_diag,
            zero_plane,
            upper_off[index_of_row] * inverse_diag,
            pivot_ratio,
        )
        transfer = compose_maps(transfer, step_map)
    incoming = prefix(
        (transfer[0], transfer[1], transfer[2], transfer[3], transfer[4], transfer[5]),
        "rad",
        compose_maps,
        (unit_plane, zero_plane, zero_plane, unit_plane, zero_plane, zero_plane),
        False,
    )
    running_g_term = incoming[2]
    running_h_term = incoming[4]
    eliminated_g_term = []
    eliminated_h_term = []
    for index_of_row in range(number_lines_total):
        denominator = diagonal[index_of_row] - lower_off[index_of_row] * running_h_term
        running_g_term = (
            right_side[index_of_row] - lower_off[index_of_row] * running_g_term
        ) / denominator
        running_h_term = upper_off[index_of_row] / denominator
        eliminated_g_term = eliminated_g_term + [running_g_term]
        eliminated_h_term = eliminated_h_term + [running_h_term]
    current_offset = eliminated_g_term[number_lines_total - 1]
    current_slope = -eliminated_h_term[number_lines_total - 1]
    offsets = [current_offset]
    slopes = [current_slope]
    for index_of_row in range(number_lines_total - 2, -1, -1):
        current_offset = (
            eliminated_g_term[index_of_row] - eliminated_h_term[index_of_row] * current_offset
        )
        current_slope = -eliminated_h_term[index_of_row] * current_slope
        offsets = [current_offset] + offsets
        slopes = [current_slope] + slopes
    through = prefix(
        (current_offset, current_slope), "rad", compose_affine, (zero_plane, unit_plane), True
    )
    beyond = through[0]
    return jnp.stack(
        [
            offsets[index_of_row] + slopes[index_of_row] * beyond
            for index_of_row in range(number_lines_total)
        ]
    )


def line_sweep(widened, extra_pivot_entry, transport_factor, source_field, geometry):
    lower_off, upper_off, radial_diag, azimuth_coef = geometry
    old_center = widened[:, 1:-1]
    side_sum = widened[:, :-2] + widened[:, 2:]
    right_side = explicit_rhs(old_center, side_sum, azimuth_coef, transport_factor, source_field)
    diagonal = radial_diag[:, None, None] + 2.0 * azimuth_coef[:, None, None] + extra_pivot_entry
    return solve_lines(lower_off, diagonal, upper_off, right_side)


def body(
    relative_base_heat,
    base_deformation_size,
    base_streamwise_flux,
    goal_heat_change,
    initial_costate_heat,
):
    number_lines_total = relative_base_heat.shape[0]
    total_rows = number_lines_total * lax.axis_size("rad")
    first_row = lax.axis_index("rad") * number_lines_total
    geometry = line_geometry(first_row, number_lines_total, total_rows, number_lines_total)
    polymer_resistance, transport_factor, extra_pivot_entry = plate_arrays(
        relative_base_heat, base_deformation_size, base_streamwise_flux
    )
    sequence_ordinal = initial_costate_heat
    for sweep_index in range(2):
        widened = padded(sequence_ordinal, (("azi", 1),), 1)
        sequence_ordinal = line_sweep(
            widened, extra_pivot_entry, transport_factor, goal_heat_change, geometry
        )
    lengthwise_velocity_sensitivity = sequence_ordinal * velocity_factor(
        relative_base_heat, polymer_resistance, base_deformation_size
    )
    return (sequence_ordinal, lengthwise_velocity_sensitivity)


def solution(mesh):
    return jax.shard_map(
        body,
        mesh=mesh,
        in_specs=(
            P("rad", "azi", None),
            P("rad", "azi", None),
            P("rad", "azi", None),
            P("rad", "azi", None),
            P("rad", "azi", None),
        ),
        out_specs=(P("rad", "azi", None), P("rad", "azi", None)),
        check_vma=False,
    )
```

profile of v0, /device:TPU:0, one launch (start us, length us, event | category | flops | bytes accessed | tf_op | source)
XLA Modules:
  0.0 321.7 jit_solution(7660898202691403454)
XLA Ops:
  0.6 1.1 fusion.98
  2.2 4.1 %collective-permute-start.1 = (f32[16,1,512]{2,1,0:T(1,128)S(1)}, f32[16,1,512]{2,1,0:T(1,128)S(1)}, u32[]{:S(2)}, u32[]{:S(2)}) collective-permute-start(f32[16,1,512]{2,1,0:T(1,128)S(1)} %get-tuple-element.809), channel_id=1, source_target_pairs={{1,0},{2,1},{3,2},{4,3},{5,4},{6,5},{7,6},{0,7},{9,8},{10,9},{11,1... | collective-permute-start | bytes 98312 | tf_op jit(solution)/shard_map/ppermute | solution.py:42
  6.3 3.3 %fusion.97 = (f32[16,32,511]{2,1,0:T(8,128)}, f32[16,32,511]{2,1,0:T(8,128)}) fusion(f32[16,32,512]{2,1,0:T(8,128)} %param.17), kind=kLoop, calls=%fused_computation.401 | loop fusion | bytes 4186112 | tf_op jit(solution)/shard_map/slice | solution.py:80
  11.1 1.3 slice_subtract_fusion
  22.5 4.8 %add_add_fusion = (f32[16,32,512]{2,1,0:T(8,128)S(1)}, f32[16,32,512]{2,1,0:T(8,128)S(1)}) fusion(f32[16,32,512]{2,1,0:T(8,128)} %param.14, f32[16,32,512]{2,1,0:T(8,128)} %param.15, f32[16,32,512]{2,1,0:T(8,128)S(1)} %copy-done, f32[16]{0:T(128)S(1)} %get-tuple-element.844, f32[16,32,512]{2,1,0:T(8,128)} %param.17, f32[16,32,511]{2,1,0:T(8,128)} %get-tuple-element.807, ...), kind=kLoop, calls=%fused_computation.50 | loop fusion | flops 5242880 | bytes 9498752 | tf_op jit(solution)/shard_map/add | solution.py:188
  27.3 10.5 %add_multiply_fusion.2 = (f32[1,32,512]{2,1,0:T(8,128)S(1)}, f32[1,32,512]{2,1,0:T(8,128)S(1)}, f32[1,32,512]{2,1,0:T(8,128)S(1)}, f32[1,32,512]{2,1,0:T(8,128)S...) fusion(f32[]{:T(128)} %bitcast.32, f32[]{:T(128)} %bitcast.31, f32[]{:T(128)S(6)} %neg.157, f32[]{:T(128)S(6)} %neg.156, ...), kind=kLoop, calls=%fused_computation.240 | loop fusion | flops 2326528 | bytes 1441920 | tf_op jit(solution)/shard_map/mul | solution.py:114
  37.8 10.6 %add_multiply_fusion.3 = f32[1,32,512]{2,1,0:T(8,128)S(1)} fusion(f32[1,32,512]{2,1,0:T(8,128)S(1)} %get-tuple-element.795, f32[1,32,512]{2,1,0:T(8,128)S(1)} %get-tuple-element.794, f32[1,32,512]{2,1,0:T(8,128)S(1)} %get-tuple-element.793, f32[1,32,512]{2,1,0:T(8,128)S(1)} %get-tuple-element.792, f32[]{:T(128)} %bitcast.32, f32[]{:T(128)} %bitcast.31, ...), kind=kLoop, calls=%fused_computation.241 | loop fusion | flops 3751936 | bytes 1441920 | tf_op jit(solution)/shard_map/mul | solution.py:113
  48.5 10.0 %add_multiply_fusion.4 = f32[1,32,512]{2,1,0:T(8,128)S(1)} fusion(f32[1,32,512]{2,1,0:T(8,128)S(1)} %get-tuple-element.795, f32[1,32,512]{2,1,0:T(8,128)S(1)} %get-tuple-element.794, f32[1,32,512]{2,1,0:T(8,128)S(1)} %get-tuple-element.793, f32[1,32,512]{2,1,0:T(8,128)S(1)} %get-tuple-element.792, f32[]{:T(128)} %bitcast.31, f32[]{:T(128)} %bitcast.30, ...), kind=kLoop, calls=%fused_computation.242 | loop fusion | flops 3719168 | bytes 1441916 | tf_op jit(solution)/shard_map/mul | solution.py:115
  58.5 6.9 %add_multiply_fusion.5 = f32[1,32,512]{2,1,0:T(8,128)S(1)} fusion(f32[1,32,512]{2,1,0:T(8,128)S(1)} %get-tuple-element.795, f32[1,32,512]{2,1,0:T(8,128)S(1)} %get-tuple-element.794, f32[1,32,512]{2,1,0:T(8,128)S(1)} %get-tuple-element.793, f32[1,32,512]{2,1,0:T(8,128)S(1)} %get-tuple-element.792, f32[1,32,512]{2,1,0:T(8,128)S(1)} %get-tuple-element.791, ...), kind=kLoop, calls=%fused_computation.243 | loop fusion | flops 3309568 | bytes 2490472 | tf_op jit(solution)/shard_map/mul | solution.py:112
  65.3 10.2 %add_multiply_fusion.6 = f32[1,32,512]{2,1,0:T(8,128)S(1)} fusion(f32[1,32,512]{2,1,0:T(8,128)S(1)} %get-tuple-element.795, f32[1,32,512]{2,1,0:T(8,128)S(1)} %get-tuple-element.794, f32[1,32,512]{2,1,0:T(8,128)S(1)} %get-tuple-element.793, f32[1,32,512]{2,1,0:T(8,128)S(1)} %get-tuple-element.792, f32[]{:T(128)} %bitcast.31, f32[]{:T(128)} %bitcast.30, ...), kind=kLoop, calls=%fused_computation.244 | loop fusion | flops 5226496 | bytes 2490492 | tf_op jit(solution)/shard_map/mul | solution.py:111
  75.5 6.7 %multiply_multiply_fusion.2 = f32[1,32,512]{2,1,0:T(8,128)S(1)} fusion(f32[1,32,512]{2,1,0:T(8,128)S(1)} %get-tuple-element.795, f32[1,32,512]{2,1,0:T(8,128)S(1)} %get-tuple-element.794, f32[1,32,512]{2,1,0:T(8,128)S(1)} %get-tuple-element.793, f32[1,32,512]{2,1,0:T(8,128)S(1)} %get-tuple-element.792, f32[]{:T(128)} %bitcast.20, f32[]{:T(128)} %bitcast.19, ...), kind=kLoop, calls=%fused_computation.276 | loop fusion | flops 2441216 | bytes 1441896 | tf_op jit(solution)/shard_map/mul | solution.py:110
  82.3 10.5 %all_gather.68 = f32[4,32,512]{2,1,0:T(8,128)} all-gather(f32[1,32,512]{2,1,0:T(8,128)S(1)} %add_multiply_fusion.3), channel_id=1, replica_groups=mesh['rad'=4,'azi'=8] {'rad'}, dimensions={0}, use_global_device_ids=true | all-gather | bytes 327680 | tf_op jit(solution)/shard_map/all_gather | solution.py:18
  92.7 9.3 %all_gather.67 = f32[4,32,512]{2,1,0:T(8,128)} all-gather(f32[1,32,512]{2,1,0:T(8,128)S(1)} %add_multiply_fusion.4), channel_id=1, replica_groups=mesh['rad'=4,'azi'=8] {'rad'}, dimensions={0}, use_global_device_ids=true | all-gather | bytes 327680 | tf_op jit(solution)/shard_map/all_gather | solution.py:18
  102.0 9.5 %all_gather.66 = f32[4,32,512]{2,1,0:T(8,128)} all-gather(f32[1,32,512]{2,1,0:T(8,128)S(1)} %add_multiply_fusion.5), channel_id=1, replica_groups=mesh['rad'=4,'azi'=8] {'rad'}, dimensions={0}, use_global_device_ids=true | all-gather | bytes 327680 | tf_op jit(solution)/shard_map/all_gather | solution.py:18
  111.5 9.1 %all_gather.65 = f32[4,32,512]{2,1,0:T(8,128)} all-gather(f32[1,32,512]{2,1,0:T(8,128)S(1)} %add_multiply_fusion.6), channel_id=1, replica_groups=mesh['rad'=4,'azi'=8] {'rad'}, dimensions={0}, use_global_device_ids=true | all-gather | bytes 327680 | tf_op jit(solution)/shard_map/all_gather | solution.py:18
  120.5 9.2 %all_gather.64 = f32[4,32,512]{2,1,0:T(8,128)} all-gather(f32[1,32,512]{2,1,0:T(8,128)S(1)} %multiply_multiply_fusion.2), channel_id=1, replica_groups=mesh['rad'=4,'azi'=8] {'rad'}, dimensions={0}, use_global_device_ids=true | all-gather | bytes 327680 | tf_op jit(solution)/shard_map/all_gather | solution.py:18
  129.7 9.1 %all_gather.69 = f32[4,32,512]{2,1,0:T(8,128)} all-gather(f32[1,32,512]{2,1,0:T(8,128)S(1)} %get-tuple-element.790), channel_id=1, replica_groups=mesh['rad'=4,'azi'=8] {'rad'}, dimensions={0}, use_global_device_ids=true | all-gather | bytes 327680 | tf_op jit(solution)/shard_map/all_gather | solution.py:18
  138.8 5.3 %while.60 = (s32[]{:T(128)}, f32[32,512]{1,0:T(8,128)}, f32[32,512]{1,0:T(8,128)}, s32[]{:T(128)}, f32[4,32,512]{2,1,0:T(8,128)}, /*index=5*/f32[4,32,512]{2,1,0...) while((s32[]{:T(128)}, f32[32,512]{1,0:T(8,128)}, ...), condition=%wide.region_1.2_spmd.clone, body=%wide.region_0.1_spmd.clone.sunk | while | flops 245764 | bytes 655501 | solution.py:30
  138.8 1.7 fusion.105
  140.5 1.8 fusion.105
  142.3 1.8 fusion.105
  144.1 21.9 %negate_multiply_fusion.27 = (f32[32,512]{1,0:T(8,128)}, f32[32,512]{1,0:T(8,128)}, f32[32,512]{1,0:T(8,128)}, f32[32,512]{1,0:T(8,128)}, f32[32,512]{1,0:T(8,12...) fusion(f32[]{:T(128)} %bitcast.2, ...), kind=kLoop, calls=%fused_computation.224 | loop fusion | flops 1261568 | bytes 2621568 | tf_op jit(solution)/shard_map/mul | solution.py:168
  166.1 8.3 %fusion.49 = (f32[32,512]{1,0:T(8,128)S(1)}, f32[32,512]{1,0:T(8,128)S(1)}, f32[32,512]{1,0:T(8,128)S(1)}, f32[32,512]{1,0:T(8,128)S(1)}, f32[32,512]{1,0:T(8,12...) fusion(f32[16,32,512]{2,1,0:T(8,128)S(1)} %get-tuple-element.80, ...), kind=kLoop, calls=%fused_computation.131 | loop fusion | flops 1064960 | bytes 3473460 | tf_op jit(solution)/shard_map/div | solution.py:154
  174.6 3.0 multiply_subtract_fusion.15
  177.6 9.1 %all-gather = f32[128,512]{1,0:T(8,128)} all-gather(f32[32,512]{1,0:T(8,128)S(1)} %get-tuple-element.767), channel_id=2, replica_groups=mesh['rad'=4,'azi'=8] {'rad'}, dimensions={0}, use_global_device_ids=true | all-gather | bytes 327680 | tf_op jit(solution)/shard_map/all_gather | solution.py:18
  186.7 1.7 rev.12
  188.4 9.5 %all-gather.1 = f32[128,512]{1,0:T(8,128)} all-gather(f32[32,512]{1,0:T(8,128)} %get-tuple-element.744), channel_id=3, replica_groups=mesh['rad'=4,'azi'=8] {'rad'}, dimensions={0}, use_global_device_ids=true | all-gather | bytes 327680 | tf_op jit(solution)/shard_map/all_gather | solution.py:18
  198.0 1.7 rev.13
  199.6 2.8 while.61
  199.6 0.9 fusion.106
  200.6 0.9 fusion.106
  201.5 0.9 fusion.106
  202.5 0.9 constant_dynamic-update-slice_fusion.15
  204.5 0.8 copy-done.31
  205.5 0.8 copy-done.29
  207.4 0.8 copy-done.25
  208.4 0.8 copy-done.43
  209.3 0.8 copy-done.41
  210.2 1.3 constant_dynamic-update-slice_fusion
  211.7 3.5 %collective-permute-start.3 = (f32[16,1,512]{2,1,0:T(1,128)S(1)}, f32[16,1,512]{2,1,0:T(1,128)S(1)}, u32[]{:S(2)}, u32[]{:S(2)}) collective-permute-start(f32[16,1,512]{2,1,0:T(1,128)S(1)} %get-tuple-element.803), channel_id=1, source_target_pairs={{1,0},{2,1},{3,2},{4,3},{5,4},{6,5},{7,6},{0,7},{9,8},{10,9},{11,1... | collective-permute-start | bytes 98312 | tf_op jit(solution)/shard_map/ppermute | solution.py:42
  215.5 1.2 collective-permute-done.2
  216.8 0.8 fusion.23
  217.6 6.9 %add_multiply_fusion = f32[1,32,512]{2,1,0:T(8,128)S(1)} fusion(f32[1,32,512]{2,1,0:T(8,128)S(1)} %copy-done.6, f32[1,32,512]{2,1,0:T(8,128)S(1)} %get-tuple-element.794, f32[1,32,512]{2,1,0:T(8,128)S(1)} %get-tuple-element.793, f32[1,32,512]{2,1,0:T(8,128)S(1)} %get-tuple-element.792, f32[1,32,512]{2,1,0:T(8,128)S(1)} %get-tuple-element.791, f32[]{:T(128)} %bitcast.31, ...), kind=kLoop, calls=%fused_computation.209 | loop fusion | flops 3309568 | bytes 2490472 | tf_op jit(solution)/shard_map/mul | solution.py:112
  224.5 10.2 %add_multiply_fusion.1 = f32[1,32,512]{2,1,0:T(8,128)S(1)} fusion(f32[1,32,512]{2,1,0:T(8,128)S(1)} %copy-done.6, f32[1,32,512]{2,1,0:T(8,128)S(1)} %get-tuple-element.794, f32[1,32,512]{2,1,0:T(8,128)S(1)} %get-tuple-element.793, f32[1,32,512]{2,1,0:T(8,128)S(1)} %get-tuple-element.792, f32[]{:T(128)} %bitcast.31, f32[]{:T(128)} %bitcast.30, f32[]{:T(128)} %bitcast.29, ...), kind=kLoop, calls=%fused_computation.210 | loop fusion | flops 5226496 | bytes 2490492 | tf_op jit(solution)/shard_map/mul | solution.py:111
  234.7 9.4 %all_gather.75 = f32[4,32,512]{2,1,0:T(8,128)} all-gather(f32[1,32,512]{2,1,0:T(8,128)S(1)} %add_multiply_fusion), channel_id=1, replica_groups=mesh['rad'=4,'azi'=8] {'rad'}, dimensions={0}, use_global_device_ids=true | all-gather | bytes 327680 | tf_op jit(solution)/shard_map/all_gather | solution.py:18
  244.2 9.2 %all_gather.74 = f32[4,32,512]{2,1,0:T(8,128)} all-gather(f32[1,32,512]{2,1,0:T(8,128)S(1)} %add_multiply_fusion.1), channel_id=1, replica_groups=mesh['rad'=4,'azi'=8] {'rad'}, dimensions={0}, use_global_device_ids=true | all-gather | bytes 327680 | tf_op jit(solution)/shard_map/all_gather | solution.py:18
  253.4 3.2 %while.62 = (s32[]{:T(128)}, f32[32,512]{1,0:T(8,128)S(1)}, f32[32,512]{1,0:T(8,128)S(1)}, s32[]{:T(128)}, f32[4,32,512]{2,1,0:T(8,128)}, /*index=5*/f32[4,32,51...) while((s32[]{:T(128)}, f32[32,512]{1,0:T(8,128)S(1)}, ...), condition=%wide.region_5.6_spmd.clone, body=%wide.region_4.5_spmd.clone.sunk | while | flops 245764 | bytes 655501 | solution.py:30
  253.4 1.1 fusion.107
  254.5 1.1 fusion.107
  255.6 1.1 fusion.107
  256.6 21.1 %negate_multiply_fusion.13 = (f32[32,512]{1,0:T(8,128)}, f32[32,512]{1,0:T(8,128)}, f32[32,512]{1,0:T(8,128)}, f32[32,512]{1,0:T(8,128)}, f32[32,512]{1,0:T(8,12...) fusion(f32[]{:T(128)} %bitcast.2, ...), kind=kLoop, calls=%fused_computation.193 | loop fusion | flops 1261568 | bytes 2621568 | tf_op jit(solution)/shard_map/mul | solution.py:168
  277.8 8.3 %fusion.33 = (f32[32,512]{1,0:T(8,128)S(1)}, f32[32,512]{1,0:T(8,128)S(1)}, f32[32,512]{1,0:T(8,128)S(1)}, f32[32,512]{1,0:T(8,128)S(1)}, f32[32,512]{1,0:T(8,12...) fusion(f32[16,32,512]{2,1,0:T(8,128)S(1)} %fusion.23, ...), kind=kLoop, calls=%fused_computation.91 | loop fusion | flops 1064960 | bytes 3473460 | tf_op jit(solution)/shard_map/div | solution.py:154
  286.2 3.0 multiply_subtract_fusion
  289.2 9.2 %all-gather.2 = f32[128,512]{1,0:T(8,128)} all-gather(f32[32,512]{1,0:T(8,128)S(1)} %get-tuple-element.721), channel_id=4, replica_groups=mesh['rad'=4,'azi'=8] {'rad'}, dimensions={0}, use_global_device_ids=true | all-gather | bytes 327680 | tf_op jit(solution)/shard_map/all_gather | solution.py:18
  298.4 1.0 rev.14
  299.4 9.1 %all-gather.3 = f32[128,512]{1,0:T(8,128)} all-gather(f32[32,512]{1,0:T(8,128)S(1)} %copy-done.44), channel_id=5, replica_groups=mesh['rad'=4,'azi'=8] {'rad'}, dimensions={0}, use_global_device_ids=true | all-gather | bytes 327680 | tf_op jit(solution)/shard_map/all_gather | solution.py:18
  308.5 1.7 rev.15
  310.2 2.7 while.63
  310.2 0.9 fusion.108
  311.1 0.9 fusion.108
  312.0 0.9 fusion.108
  312.9 0.9 constant_dynamic-update-slice_fusion.31
  318.8 1.3 constant_dynamic-update-slice_fusion.16
  320.2 1.5 subtract_multiply_fusion
  (246 shorter events, 9.8 us)
Async XLA Ops:
  1.7 20.8 %collective-permute-start = (f32[16,1,512]{2,1,0:T(1,128)S(1)}, f32[16,1,512]{2,1,0:T(1,128)S(1)}, u32[]{:S(2)}, u32[]{:S(2)}) collective-permute-start(f32[16,1,512]{2,1,0:T(1,128)S(1)} %get-tuple-element.808), channel_id=1, source_target_pairs={{0,1},{1,2},{2,3},{3,4},{4,5},{5,6},{6,7},{7,0},{8,9},{9,10},{10,1... | collective-permute-start | bytes 98312 | tf_op jit(solution)/shard_map/ppermute | solution.py:39
  2.2 20.3 %collective-permute-start.1 = (f32[16,1,512]{2,1,0:T(1,128)S(1)}, f32[16,1,512]{2,1,0:T(1,128)S(1)}, u32[]{:S(2)}, u32[]{:S(2)}) collective-permute-start(f32[16,1,512]{2,1,0:T(1,128)S(1)} %get-tuple-element.809), channel_id=1, source_target_pairs={{1,0},{2,1},{3,2},{4,3},{5,4},{6,5},{7,6},{0,7},{9,8},{10,9},{11,1... | collective-permute-start | bytes 98312 | tf_op jit(solution)/shard_map/ppermute | solution.py:42
  6.3 4.8 %copy-start = (f32[16,32,512]{2,1,0:T(8,128)S(1)}, f32[16,32,512]{2,1,0:T(8,128)}, u32[]{:S(2)}) copy-start(f32[16,32,512]{2,1,0:T(8,128)} %param.13) | copy-start | bytes 3145732
  37.8 37.7 %copy-start.5 = (f32[1,32,512]{2,1,0:T(8,128)}, f32[1,32,512]{2,1,0:T(8,128)S(1)}, u32[]{:S(2)}) copy-start(f32[1,32,512]{2,1,0:T(8,128)S(1)} %get-tuple-element.795) | copy-start | bytes 196612
  144.1 22.0 %copy-start.8 = (f32[32,512]{1,0:T(8,128)S(1)}, f32[32,512]{1,0:T(8,128)}, u32[]{:S(2)}) copy-start(f32[32,512]{1,0:T(8,128)} %get-tuple-element.531) | copy-start | bytes 196612
  144.1 22.0 %copy-start.10 = (f32[32,512]{1,0:T(8,128)S(1)}, f32[32,512]{1,0:T(8,128)}, u32[]{:S(2)}) copy-start(f32[32,512]{1,0:T(8,128)} %get-tuple-element.530) | copy-start | bytes 196612
  166.0 8.5 %copy-start.24 = (f32[32,512]{1,0:T(8,128)}, f32[32,512]{1,0:T(8,128)S(1)}, u32[]{:S(2)}) copy-start(f32[32,512]{1,0:T(8,128)S(1)} %get-tuple-element.755) | copy-start | bytes 196612
  166.0 8.5 %copy-start.26 = (f32[32,512]{1,0:T(8,128)}, f32[32,512]{1,0:T(8,128)S(1)}, u32[]{:S(2)}) copy-start(f32[32,512]{1,0:T(8,128)S(1)} %get-tuple-element.757) | copy-start | bytes 196612
  166.0 8.5 %copy-start.28 = (f32[32,512]{1,0:T(8,128)}, f32[32,512]{1,0:T(8,128)S(1)}, u32[]{:S(2)}) copy-start(f32[32,512]{1,0:T(8,128)S(1)} %get-tuple-element.759) | copy-start | bytes 196612
  166.0 8.5 %copy-start.30 = (f32[32,512]{1,0:T(8,128)}, f32[32,512]{1,0:T(8,128)S(1)}, u32[]{:S(2)}) copy-start(f32[32,512]{1,0:T(8,128)S(1)} %get-tuple-element.761) | copy-start | bytes 196612
  166.0 8.5 %copy-start.32 = (f32[32,512]{1,0:T(8,128)}, f32[32,512]{1,0:T(8,128)S(1)}, u32[]{:S(2)}) copy-start(f32[32,512]{1,0:T(8,128)S(1)} %get-tuple-element.763) | copy-start | bytes 196612
  166.0 8.5 %copy-start.34 = (f32[32,512]{1,0:T(8,128)}, f32[32,512]{1,0:T(8,128)S(1)}, u32[]{:S(2)}) copy-start(f32[32,512]{1,0:T(8,128)S(1)} %get-tuple-element.765) | copy-start | bytes 196612
  166.1 8.5 %copy-start.40 = (f32[32,512]{1,0:T(8,128)}, f32[32,512]{1,0:T(8,128)S(1)}, u32[]{:S(2)}) copy-start(f32[32,512]{1,0:T(8,128)S(1)} %get-tuple-element.752) | copy-start | bytes 196612
  166.1 8.5 %copy-start.42 = (f32[32,512]{1,0:T(8,128)}, f32[32,512]{1,0:T(8,128)S(1)}, u32[]{:S(2)}) copy-start(f32[32,512]{1,0:T(8,128)S(1)} %get-tuple-element.753) | copy-start | bytes 196612
  174.4 3.1 copy-start.51
  174.4 3.1 copy-start.55
  174.4 3.1 copy-start.59
  174.5 3.1 copy-start.63
  174.5 3.1 copy-start.65
  174.5 3.1 copy-start.67
  177.6 9.2 %copy-start.70 = (f32[32,512]{1,0:T(8,128)}, f32[32,512]{1,0:T(8,128)S(1)}, u32[]{:S(2)}) copy-start(f32[32,512]{1,0:T(8,128)S(1)} %get-tuple-element.767) | copy-start | bytes 196612
  202.4 1.0 copy-start.35
  202.4 1.0 copy-start.68
  202.4 1.0 copy-start.88
  202.4 1.0 copy-start.98
  211.6 5.2 %collective-permute-start.2 = (f32[16,1,512]{2,1,0:T(1,128)S(1)}, f32[16,1,512]{2,1,0:T(1,128)S(1)}, u32[]{:S(2)}, u32[]{:S(2)}) collective-permute-start(f32[16,1,512]{2,1,0:T(1,128)S(1)} %get-tuple-element.802), channel_id=1, source_target_pairs={{0,1},{1,2},{2,3},{3,4},{4,5},{5,6},{6,7},{7,0},{8,9},{9,10},{10,1... | collective-permute-start | bytes 98312 | tf_op jit(solution)/shard_map/ppermute | solution.py:39
  211.6 5.1 %copy-start.1 = (f32[16,32,512]{2,1,0:T(8,128)S(1)}, f32[16,32,512]{2,1,0:T(8,128)}, u32[]{:S(2)}) copy-start(f32[16,32,512]{2,1,0:T(8,128)} %param.15) | copy-start | bytes 3145732
  211.6 5.1 %copy-start.2 = (f32[16,32,512]{2,1,0:T(8,128)S(1)}, f32[16,32,512]{2,1,0:T(8,128)}, u32[]{:S(2)}) copy-start(f32[16,32,512]{2,1,0:T(8,128)} %param.16) | copy-start | bytes 3145732
  211.7 5.1 %collective-permute-start.3 = (f32[16,1,512]{2,1,0:T(1,128)S(1)}, f32[16,1,512]{2,1,0:T(1,128)S(1)}, u32[]{:S(2)}, u32[]{:S(2)}) collective-permute-start(f32[16,1,512]{2,1,0:T(1,128)S(1)} %get-tuple-element.803), channel_id=1, source_target_pairs={{1,0},{2,1},{3,2},{4,3},{5,4},{6,5},{7,6},{0,7},{9,8},{10,9},{11,1... | collective-permute-start | bytes 98312 | tf_op jit(solution)/shard_map/ppermute | solution.py:42
  244.1 9.2 %copy-start.7 = (f32[32,512]{1,0:T(8,128)S(1)}, f32[32,512]{1,0:T(8,128)}, u32[]{:S(2)}) copy-start(f32[32,512]{1,0:T(8,128)} %custom-call.4) | copy-start | bytes 196612
  244.1 9.2 %copy-start.9 = (f32[32,512]{1,0:T(8,128)S(1)}, f32[32,512]{1,0:T(8,128)}, u32[]{:S(2)}) copy-start(f32[32,512]{1,0:T(8,128)} %custom-call.3) | copy-start | bytes 196612
  277.7 8.4 %copy-start.12 = (f32[32,512]{1,0:T(8,128)}, f32[32,512]{1,0:T(8,128)S(1)}, u32[]{:S(2)}) copy-start(f32[32,512]{1,0:T(8,128)S(1)} %get-tuple-element.709) | copy-start | bytes 196612
  277.7 8.4 %copy-start.14 = (f32[32,512]{1,0:T(8,128)}, f32[32,512]{1,0:T(8,128)S(1)}, u32[]{:S(2)}) copy-start(f32[32,512]{1,0:T(8,128)S(1)} %get-tuple-element.711) | copy-start | bytes 196612
  277.7 8.5 %copy-start.16 = (f32[32,512]{1,0:T(8,128)}, f32[32,512]{1,0:T(8,128)S(1)}, u32[]{:S(2)}) copy-start(f32[32,512]{1,0:T(8,128)S(1)} %get-tuple-element.713) | copy-start | bytes 196612
  277.7 8.5 %copy-start.18 = (f32[32,512]{1,0:T(8,128)}, f32[32,512]{1,0:T(8,128)S(1)}, u32[]{:S(2)}) copy-start(f32[32,512]{1,0:T(8,128)S(1)} %get-tuple-element.715) | copy-start | bytes 196612
  277.7 8.5 %copy-start.20 = (f32[32,512]{1,0:T(8,128)}, f32[32,512]{1,0:T(8,128)S(1)}, u32[]{:S(2)}) copy-start(f32[32,512]{1,0:T(8,128)S(1)} %get-tuple-element.717) | copy-start | bytes 196612
  277.7 8.5 %copy-start.22 = (f32[32,512]{1,0:T(8,128)}, f32[32,512]{1,0:T(8,128)S(1)}, u32[]{:S(2)}) copy-start(f32[32,512]{1,0:T(8,128)S(1)} %get-tuple-element.719) | copy-start | bytes 196612
  277.7 8.5 %copy-start.36 = (f32[32,512]{1,0:T(8,128)}, f32[32,512]{1,0:T(8,128)S(1)}, u32[]{:S(2)}) copy-start(f32[32,512]{1,0:T(8,128)S(1)} %get-tuple-element.706) | copy-start | bytes 196612
  277.7 8.5 %copy-start.38 = (f32[32,512]{1,0:T(8,128)}, f32[32,512]{1,0:T(8,128)S(1)}, u32[]{:S(2)}) copy-start(f32[32,512]{1,0:T(8,128)S(1)} %get-tuple-element.707) | copy-start | bytes 196612
  286.1 3.1 copy-start.45
  286.1 3.1 copy-start.47
  286.1 3.1 copy-start.49
  286.1 3.1 copy-start.53
  286.1 3.1 copy-start.57
  286.1 3.1 copy-start.61
  289.2 9.2 %copy-start.69 = (f32[32,512]{1,0:T(8,128)}, f32[32,512]{1,0:T(8,128)S(1)}, u32[]{:S(2)}) copy-start(f32[32,512]{1,0:T(8,128)S(1)} %get-tuple-element.721) | copy-start | bytes 196612
  298.4 1.0 copy-start.44
  312.9 1.0 copy-start.23
  312.9 1.0 copy-start.62
  312.9 1.0 copy-start.78
  312.9 1.0 copy-start.97
  316.8 1.1 copy-start.85
  316.8 1.2 copy-start.82
  316.8 1.2 copy-start.101
  316.9 2.0 copy-start.99
  316.9 0.9 copy-start.15
  316.9 0.9 copy-start.48
  316.9 1.0 copy-start.13
  316.9 1.0 copy-start.46
  316.9 1.0 copy-start.72
  317.9 1.0 copy-start.37
  317.9 2.3 copy-start.4
  317.9 2.3 copy-start.3
  320.2 1.5 copy-start.11
  (43 other events, 37.5 us)
where the time goes:
time: 326 us; the launch traced here: 322 us
  other arithmetic  165 us (51%)
  blocking collectives  112 us (34%)
  local copies, waits for them, and re-layouts  22.9 us (7%)
  between operations  12 us (4%)
  starting transfers between devices  8.18 us (3%)
    all_gather x12, blocking collectives, prefix(): pieces = jax.tree.map(lambda part: lax.all_gather(part, axis), value)  112 us
    mul x2, other arithmetic, solve_lines(): current_slope = -eliminated_h_term[index_of_row] * current_slope  43 us
    mul x2, other arithmetic, compose_maps(): second_entry * inverse_norm  20.3 us
    div x2, other arithmetic, solve_lines(): (right_side[index_of_row] - lower_off[index_of_row] * running_g_term) / d...  16.6 us
    select_n x12, other arithmetic, lap(): jnp.where(position < mine, new, old)  13.8 us
    mul x2, other arithmetic, compose_maps(): third_entry * inverse_norm  13.8 us
    mul x1, other arithmetic, compose_maps(): fourth_entry * inverse_norm  10.6 us
    unnamed x206, local copies, waits for them, and re-layouts  10.6 us
  transfers between devices with their start and end apart: 4, of which 1 were waited for; matrix products, arithmetic and copies ran while one was open for 2% of the time, Pallas kernels for 0%

commit v1 on v0

v1 whole, which is shorter than its diff:
```python
import functools

import jax
import jax.numpy as jnp
from jax import lax
from jax.experimental import pallas as pl
from jax.experimental.pallas import tpu as pltpu
from jax.sharding import PartitionSpec as P

radial_weight = 8.0
azimuth_weight = 0.25
axial_weight = 0.25
flow_weight = 0.5
mass_weight = 1.0
heat_weight = 0.25
arrhenius_exponent = 2.0
slope_weight = 2.0

MESH = pl.DeviceIdType.MESH
LANES = 128
SUB = 8


def kernel(
    segments,
    sectors,
    heat_hbm,
    size_hbm,
    flux_hbm,
    goal_hbm,
    start_hbm,
    adjoint_hbm,
    sens_hbm,
    heat,
    size,
    flux,
    goal,
    state,
    inv,
    qa,
    rb,
    rhs,
    part,
    out_x,
    out_s,
    halo_out,
    halo_in,
    coef_out,
    coef_in,
    u_out,
    u_in,
    ret_out,
    ret_in,
    in_sem,
    out_sem,
    halo_ssem,
    halo_rsem,
    coef_ssem,
    coef_rsem,
    u_ssem,
    u_rsem,
    ret_ssem,
    ret_rsem,
):
    rows, width, axial = heat.shape
    groups = width // SUB
    chunks = axial // LANES
    per_chunk = segments // chunks
    tile_rows = width // per_chunk
    total = rows * segments
    stiffness = radial_weight * rows * rows

    seg = lax.axis_index("rad")
    sec = lax.axis_index("azi")
    above = lax.rem(sec + 1, sectors)
    below = lax.rem(sec + sectors - 1, sectors)
    peers = [lax.rem(seg + k, segments) for k in range(1, segments)]
    first = seg * rows

    loads = [
        pltpu.make_async_copy(src, dst, in_sem.at[n])
        for n, (src, dst) in enumerate(
            (
                (start_hbm, state),
                (heat_hbm, heat),
                (size_hbm, size),
                (flux_hbm, flux),
                (goal_hbm, goal),
            )
        )
    ]
    for load in loads:
        load.start()

    barrier = pltpu.get_barrier_semaphore()
    for peer in peers:
        pl.semaphore_signal(barrier, inc=1, device_id=(peer, sec), device_id_type=MESH)
    for near in (above, below):
        pl.semaphore_signal(barrier, inc=1, device_id=(seg, near), device_id_type=MESH)

    def halo_copies(sweep):
        return [
            pltpu.make_async_remote_copy(
                src_ref=halo_out.at[sweep, side],
                dst_ref=halo_in.at[sweep, side],
                send_sem=halo_ssem.at[sweep, side],
                recv_sem=halo_rsem.at[sweep, side],
                device_id=(seg, near),
                device_id_type=MESH,
            )
            for side, near in ((0, above), (1, below))
        ]

    def sends(src, dst, ssem, rsem):
        return [
            pltpu.make_async_remote_copy(
                src_ref=src.at[peer],
                dst_ref=dst.at[seg],
                send_sem=ssem.at[peer],
                recv_sem=rsem.at[seg],
                device_id=(peer, sec),
                device_id_type=MESH,
            )
            for peer in peers
        ]

    def await_from(src, dst, ssem, rsem):
        for peer in peers:
            pltpu.make_async_remote_copy(
                src_ref=src.at[peer],
                dst_ref=dst.at[peer],
                send_sem=ssem.at[peer],
                recv_sem=rsem.at[peer],
                device_id=(peer, sec),
                device_id_type=MESH,
            ).wait_recv()

    def geometry(i):
        row = (first + i).astype(jnp.float32)
        radius = 1.0 + (row + 0.5) * (1.0 / total)
        low = stiffness * (1.0 + row * (1.0 / total))
        high = stiffness * (1.0 + (row + 1.0) * (1.0 / total))
        return radius, low, high

    def azimuth_coef(radius):
        return azimuth_weight / jnp.full((1, LANES), radius, jnp.float32)

    def wide(line):
        return jnp.concatenate([line] * chunks, axis=1)

    loads[0].wait()

    def pack(i, carry):
        halo_out[0, 0, pl.ds(i, 1), :] = state[i, width - 1 : width, :]
        halo_out[0, 1, pl.ds(i, 1), :] = state[i, 0:1, :]
        return carry

    lax.fori_loop(0, rows, pack, 0, unroll=4)
    pl.semaphore_wait(barrier, segments + 1)
    halos = halo_copies(0)
    for copy in halos:
        copy.start()

    for load in loads[1:4]:
        load.wait()

    def pieces():
        for c in range(chunks):
            for k in range(per_chunk):
                yield c * per_chunk + k, slice(k * tile_rows, (k + 1) * tile_rows), c

    def scatter(ref, slot, plane, c_first, c_last):
        for owner, where_rows, c in pieces():
            if c_first <= c < c_last:
                at = (c - c_first) * LANES
                ref[owner, slot] = plane[where_rows, at : at + LANES]

    half = 2 * LANES
    for h in range(axial // half):
        cols = slice(h * half, (h + 1) * half)

        def eliminate(i, carry):
            ratio, ea, prod, va, _ = carry
            radius, low, high = geometry(i)
            az2 = 2.0 * azimuth_coef(radius)
            az2 = jnp.concatenate([az2, az2], axis=1)
            viscosity = jnp.exp(
                arrhenius_exponent - arrhenius_exponent * heat[i, :, cols]
            )
            extent = size[i, :, cols]
            shear = (heat_weight * arrhenius_exponent) * viscosity * extent
            ahead = radius * (axial_weight + flow_weight * flux[i, :, cols])
            excess = (
                ahead + radius * (shear * extent + (mass_weight + axial_weight)) + az2
            )
            top = low * ratio + excess
            inverse = 1.0 / (top + high)
            ratio = top * inverse
            ea = (low * inverse) * ea
            upper = high * inverse
            va = va + prod * ea
            prod = prod * upper
            flux[i, :, cols] = ahead
            size[i, :, cols] = shear
            inv[i, :, cols] = inverse
            qa[i, :, cols] = ea
            return ratio, ea, prod, va, upper

        one = jnp.ones((width, half), jnp.float32)
        zero = jnp.zeros((width, half), jnp.float32)
        _, ea, _, va, upper = lax.fori_loop(
            0, rows, eliminate, (one, one, one, zero, zero)
        )
        scatter(coef_out, 0, va, 2 * h, 2 * h + 2)
        scatter(coef_out, 1, ea, 2 * h, 2 * h + 2)
        scatter(coef_out, 2, upper, 2 * h, 2 * h + 2)

    coef_sends = sends(coef_out, coef_in, coef_ssem, coef_rsem)
    for copy in coef_sends:
        copy.start()
    coef_in[seg] = coef_out[seg]

    def respond(n, carry):
        q_next, r_next = carry
        i = rows - 1 - n
        _, _, high = geometry(i)
        upper = high * inv[i]
        q_next = qa[i] + upper * q_next
        r_next = upper * r_next
        qa[i] = q_next
        rb[i] = r_next
        return q_next, r_next

    lax.fori_loop(
        0,
        rows,
        respond,
        (jnp.zeros((width, axial), jnp.float32), jnp.ones((width, axial), jnp.float32)),
    )

    loads[4].wait()
    sub = lax.broadcasted_iota(jnp.int32, (SUB, axial), 0)
    lane = lax.broadcasted_iota(jnp.int32, (SUB, axial), 1)

    def right_side(sweep, chosen):
        def step(i, carry):
            radius, _, _ = geometry(i)
            az = wide(azimuth_coef(radius))
            rolled_up, rolled_down, new = {}, {}, []

            def block(g):
                return state[i, g * SUB : (g + 1) * SUB, :]

            def up(g):
                if g < 0:
                    return jnp.broadcast_to(
                        halo_in[sweep, 0, pl.ds(i, 1), :], (SUB, axial)
                    )
                if g not in rolled_up:
                    rolled_up[g] = pltpu.roll(block(g), 1, 0)
                return rolled_up[g]

            def down(g):
                if g >= groups:
                    return jnp.broadcast_to(
                        halo_in[sweep, 1, pl.ds(i, 1), :], (SUB, axial)
                    )
                if g not in rolled_down:
                    rolled_down[g] = pltpu.roll(block(g), SUB - 1, 0)
                return rolled_down[g]

            for g, (u_first, u_last) in zip(chosen, carry):
                here = slice(g * SUB, (g + 1) * SUB)
                x = block(g)
                sides = jnp.where(sub == 0, up(g - 1), up(g)) + jnp.where(
                    sub == SUB - 1, down(g + 1), down(g)
                )
                before = jnp.where(lane == 0, 0.0, pltpu.roll(x, 1, 1))
                after = jnp.where(lane == axial - 1, 0.0, pltpu.roll(x, axial - 1, 1))
                value = (
                    radius * (goal[i, here, :] + mass_weight * x + axial_weight * before)
                    + flux[i, here, :] * after
                    + az * sides
                )
                rhs[i, here, :] = value
                new.append(
                    (u_first + qa[i, here, :] * value, u_last + rb[i, here, :] * value)
                )
            return tuple(new)

        zero = jnp.zeros((SUB, axial), jnp.float32)
        sums = lax.fori_loop(0, rows, step, tuple((zero, zero) for _ in chosen))
        for g, pair in zip(chosen, sums):
            for slot, plane in enumerate(pair):
                for owner, where_rows, c in pieces():
                    at = g * SUB - where_rows.start
                    if 0 <= at < tile_rows:
                        u_out[sweep, owner, slot, at : at + SUB, :] = plane[
                            :, c * LANES : (c + 1) * LANES
                        ]

    def send_ends(sweep):
        copies = sends(
            u_out.at[sweep], u_in.at[sweep], u_ssem.at[sweep], u_rsem.at[sweep]
        )
        for copy in copies:
            copy.start()
        u_in[sweep, seg] = u_out[sweep, seg]
        return copies

    def await_ends(sweep):
        await_from(u_out.at[sweep], u_in.at[sweep], u_ssem.at[sweep], u_rsem.at[sweep])

    def substitute():
        def forward(i, g):
            _, low, _ = geometry(i)
            g = inv[i] * (rhs[i] + low * g)
            rhs[i] = g
            return g

        def backward(n, p):
            i = rows - 1 - n
            _, _, high = geometry(i)
            p = rhs[i] + (high * inv[i]) * p
            part[i] = p
            return p

        zero = jnp.zeros((width, axial), jnp.float32)
        lax.fori_loop(0, rows, forward, zero)
        lax.fori_loop(0, rows, backward, zero)

    def reduced_factors():
        factors, beta = [], None
        for s in range(segments):
            v_first, v_last, w_last = coef_in[s, 0], coef_in[s, 1], coef_in[s, 2]
            w_first = v_last * ((segments + s + 1.0) / (segments + s))
            if s == 0:
                factors.append((None, None, None, w_first, w_last, None))
                beta = w_last
                continue
            scale = 1.0 / (1.0 - v_first * beta)
            q = scale * w_first
            cross = v_last * beta
            new_beta = w_last + cross * q
            factors.append((scale, scale * v_first, v_last, q, new_beta, cross))
            beta = new_beta
        return factors

    def reduced_solve(sweep, factors):
        firsts, lasts = [], []
        for s in range(segments):
            u_first = u_in[sweep, s, 0] * (segments / (stiffness * (segments + s)))
            u_last = u_in[sweep, s, 1] * (segments / (stiffness * (segments + s + 1)))
            if s == 0:
                firsts.append(u_first)
                lasts.append(u_last)
                continue
            scale, scaled_v, v_last, _, _, cross = factors[s]
            p = scale * u_first + scaled_v * lasts[s - 1]
            firsts.append(p)
            lasts.append(u_last + v_last * lasts[s - 1] + cross * p)
        blank = jnp.zeros((tile_rows, LANES), jnp.float32)
        beyond = blank
        ret_out[sweep, 0, 0] = blank
        for s in range(segments - 1, -1, -1):
            ret_out[sweep, s, 1] = beyond
            if s < segments - 1:
                ret_out[sweep, s + 1, 0] = lasts[s] + factors[s][4] * beyond
            beyond = firsts[s] + factors[s][3] * beyond if s > 0 else beyond

    def send_back(sweep):
        copies = sends(
            ret_out.at[sweep], ret_in.at[sweep], ret_ssem.at[sweep], ret_rsem.at[sweep]
        )
        for copy in copies:
            copy.start()
        ret_in[sweep, seg] = ret_out[sweep, seg]
        return copies

    def await_back(sweep):
        await_from(
            ret_out.at[sweep], ret_in.at[sweep], ret_ssem.at[sweep], ret_rsem.at[sweep]
        )

    def ends(sweep):
        planes = []
        for slot in range(2):
            planes.append(
                jnp.concatenate(
                    [
                        jnp.concatenate(
                            [
                                ret_in[sweep, c * per_chunk + k, slot]
                                for k in range(per_chunk)
                            ],
                            axis=0,
                        )
                        for c in range(chunks)
                    ],
                    axis=1,
                )
            )
        return planes

    for copy in halos:
        copy.wait_recv()
    right_side(0, tuple(range(groups)))
    started = [coef_sends, halos, send_ends(0)]
    substitute()
    await_from(coef_out, coef_in, coef_ssem, coef_rsem)
    factors = reduced_factors()
    await_ends(0)
    reduced_solve(0, factors)
    started.append(send_back(0))

    last_lane = lax.broadcasted_iota(jnp.int32, (width, axial), 1) == axial - 1

    def slope(i, carry):
        here = heat[i]
        rise = jnp.where(last_lane, 0.0, pltpu.roll(here, axial - 1, 1) - here)
        heat[i] = slope_weight * rise - size[i]
        return carry

    lax.fori_loop(0, rows, slope, 0)

    await_back(0)
    a, b = ends(0)

    def advance(i, carry):
        x = part[i] + qa[i] * a + rb[i] * b
        state[i] = x
        halo_out[1, 0, pl.ds(i, 1), :] = x[width - 1 : width, :]
        halo_out[1, 1, pl.ds(i, 1), :] = x[0:1, :]
        return carry

    lax.fori_loop(0, rows, advance, 0)
    halos = halo_copies(1)
    for copy in halos:
        copy.start()

    for copy in halos:
        copy.wait_recv()
    right_side(1, tuple(range(groups)))
    started += [halos, send_ends(1)]
    substitute()
    await_ends(1)
    reduced_solve(1, reduced_factors())
    started.append(send_back(1))
    await_back(1)
    a, b = ends(1)

    quarter = rows // 4
    stores = []
    for n in range(4):

        def finish(i, carry):
            x = part[i] + qa[i] * a + rb[i] * b
            out_x[i] = x
            out_s[i] = x * heat[i]
            return carry

        lax.fori_loop(n * quarter, (n + 1) * quarter, finish, 0)
        span = slice(n * quarter, (n + 1) * quarter)
        for m, (src, dst) in enumerate(((out_x, adjoint_hbm), (out_s, sens_hbm))):
            store = pltpu.make_async_copy(
                src.at[pl.ds(n * quarter, quarter)],
                dst.at[pl.ds(n * quarter, quarter)],
                out_sem.at[m, n],
            )
            store.start()
            stores.append(store)

    for copies in started:
        for copy in copies:
            copy.wait_send()
    for store in stores:
        store.wait()


def solution(mesh):
    segments, sectors = mesh.shape["rad"], mesh.shape["azi"]
    spec = P("rad", "azi", None)

    def body(heat, size, flux, goal, start):
        rows, width, axial = heat.shape
        tile_rows = width * axial // (segments * LANES)
        block = pltpu.VMEM((rows, width, axial), jnp.float32)
        tile = (tile_rows, LANES)
        shape = jax.ShapeDtypeStruct((rows, width, axial), jnp.float32)
        dma = pltpu.SemaphoreType.DMA
        cells = rows * width * axial
        return pl.pallas_call(
            functools.partial(kernel, segments, sectors),
            out_shape=(shape, shape),
            in_specs=[pl.BlockSpec(memory_space=pl.ANY)] * 5,
            out_specs=[pl.BlockSpec(memory_space=pl.ANY)] * 2,
            scratch_shapes=[block] * 12
            + [
                pltpu.VMEM((2, 2, rows, axial), jnp.float32),
                pltpu.VMEM((2, 2, rows, axial), jnp.float32),
                pltpu.VMEM((segments, 3) + tile, jnp.float32),
                pltpu.VMEM((segments, 3) + tile, jnp.float32),
                pltpu.VMEM((2, segments, 2) + tile, jnp.float32),
                pltpu.VMEM((2, segments, 2) + tile, jnp.float32),
                pltpu.VMEM((2, segments, 2) + tile, jnp.float32),
                pltpu.VMEM((2, segments, 2) + tile, jnp.float32),
                dma((5,)),
                dma((2, 4)),
                dma((2, 2)),
                dma((2, 2)),
                dma((segments,)),
                dma((segments,)),
                dma((2, segments)),
                dma((2, segments)),
                dma((2, segments)),
                dma((2, segments)),
            ],
            compiler_params=pltpu.CompilerParams(
                collective_id=0, has_side_effects=True, vmem_limit_bytes=32 * 2**20
            ),
            cost_estimate=pl.CostEstimate(
                flops=120 * cells, bytes_accessed=28 * cells, transcendentals=2 * cells
            ),
        )(heat, size, flux, goal, start)

    return jax.shard_map(
        body, mesh=mesh, in_specs=(spec,) * 5, out_specs=(spec, spec), check_vma=False
    )
```

time: 326 us -> 39.7 us (0.12); the launches traced: 322 us -> 39.4 us
  other arithmetic: 165 us -> 0 us
  blocking collectives: 112 us -> 0 us
  Pallas kernels: 0 us -> 30.7 us
  local copies, waits for them, and re-layouts: 22.9 us -> 8.06 us
  between operations: 12 us -> 0.65 us
  starting transfers between devices: 8.18 us -> 0 us
    mul x11 -> x0, other arithmetic: 116 us -> none  [the longest x2 43 us: solve_lines(): current_slope = -eliminated_h_term[index_of_row] * current_slope]
    all_gather x12 -> x0, blocking collectives: 112 us -> none  [prefix(): pieces = jax.tree.map(lambda part: lax.all_gather(part, axis), value)]
    pallas_call x0 -> x1, Pallas kernels: none -> 30.7 us  [body(): pl.pallas_call(functools.partial(kernel, segments, sectors), out_shape=(s...]
    div x2 -> x0, other arithmetic: 16.6 us -> none  [solve_lines(): (right_side[index_of_row] - lower_off[index_of_row] * running_g_term) / d...]
    select_n x13 -> x0, other arithmetic: 13.8 us -> none  [the longest x12 13.8 us: lap(): jnp.where(position < mine, new, old)]
    ppermute x4 -> x0, starting transfers between devices: 8.18 us -> none  [the longest x2 7.61 us: padded(): lax.ppermute(lax.slice_in_dim(block, 0, width, axis=dim), axis, backward)]
    sub x3 -> x0, other arithmetic: 7.27 us -> none  [the longest x2 5.93 us: solve_lines(): eliminated_g_term[index_of_row]]
    slice x6 -> x0, local copies, waits for them, and re-layouts: 6.26 us -> none  [the longest x2 3.7 us: explicit_rhs(): prev_cell = jnp.concatenate([edge_nulls, old_center[:, :, :-1]], axis=2)]
  transfers between devices with their start and end apart: 4 -> 0, of which waited for: 1 -> 0; matrix products, arithmetic and copies ran while one was open for 2% -> 0% of each run, Pallas kernels for 0% -> 0%
where the time goes in v1:
time: 39.7 us; the launch traced here: 39.4 us
  Pallas kernels  30.7 us (77%)
  local copies, waits for them, and re-layouts  8.06 us (20%)
  between operations  0.65 us (2%)
    pallas_call x1, Pallas kernels, body(): pl.pallas_call(functools.partial(kernel, segments, sectors), out_shape=(s...  30.7 us
    unnamed x12, local copies, waits for them, and re-layouts  8.06 us

profile of v1, /device:TPU:0, one launch (start us, length us, event | category | flops | bytes accessed | tf_op | source)
XLA Modules:
  0.0 39.4 jit_solution(14471040637139373713)
XLA Ops:
  0.6 0.0 copy-start
  0.6 1.2 %copy-done = f32[16,32,512]{2,1,0:T(8,128)S(1)} copy-done((f32[16,32,512]{2,1,0:T(8,128)S(1)}, f32[16,32,512]{2,1,0:T(8,128)}, u32[]{:S(2)}) %copy-start) | copy-done | bytes 1048600
  1.9 0.0 copy-start.1
  1.9 1.2 %copy-done.1 = f32[16,32,512]{2,1,0:T(8,128)S(1)} copy-done((f32[16,32,512]{2,1,0:T(8,128)S(1)}, f32[16,32,512]{2,1,0:T(8,128)}, u32[]{:S(2)}) %copy-start.1) | copy-done | bytes 1048600
  3.1 0.0 copy-start.2
  3.1 1.2 %copy-done.2 = f32[16,32,512]{2,1,0:T(8,128)S(1)} copy-done((f32[16,32,512]{2,1,0:T(8,128)S(1)}, f32[16,32,512]{2,1,0:T(8,128)}, u32[]{:S(2)}) %copy-start.2) | copy-done | bytes 1048600
  4.3 0.0 copy-start.3
  4.3 1.2 %copy-done.3 = f32[16,32,512]{2,1,0:T(8,128)S(1)} copy-done((f32[16,32,512]{2,1,0:T(8,128)S(1)}, f32[16,32,512]{2,1,0:T(8,128)}, u32[]{:S(2)}) %copy-start.3) | copy-done | bytes 1048600
  5.5 0.0 copy-start.4
  5.5 1.2 %copy-done.4 = f32[16,32,512]{2,1,0:T(8,128)S(1)} copy-done((f32[16,32,512]{2,1,0:T(8,128)S(1)}, f32[16,32,512]{2,1,0:T(8,128)}, u32[]{:S(2)}) %copy-start.4) | copy-done | bytes 1048600
  6.8 30.7 %shard_map.68 = (f32[16,32,512]{2,1,0:T(8,128)S(1)}, f32[16,32,512]{2,1,0:T(8,128)S(1)}) custom-call(f32[16,32,512]{2,1,0:T(8,128)S(1)} %copy-done, f32[16,32,512]{2,1,0:T(8,128)S(1)} %copy-done.1, f32[16,32,512]{2,1,0:T(8,128)S(1)} %copy-done.2, f32[16,32,512]{2,1,0:T(8,128)S(1)} %copy-done.3, f32[16,32,512]{2,1,0:T(8,128)S(1)} %copy-done.4), custom_call_target="tpu_custom_call" | custom-call | flops 31457280 | bytes 7340032 | tf_op jit(solution)/shard_map/pallas_call | solution.py:492
  37.5 1.0 %copy.9 = f32[16,32,512]{2,1,0:T(8,128)} copy(f32[16,32,512]{2,1,0:T(8,128)S(1)} %get-tuple-element.4) | data formatting | bytes 2097152
  38.5 1.0 %copy.10 = f32[16,32,512]{2,1,0:T(8,128)} copy(f32[16,32,512]{2,1,0:T(8,128)S(1)} %get-tuple-element.5) | data formatting | bytes 2097152
Async XLA Ops:
  0.6 1.2 %copy-start = (f32[16,32,512]{2,1,0:T(8,128)S(1)}, f32[16,32,512]{2,1,0:T(8,128)}, u32[]{:S(2)}) copy-start(f32[16,32,512]{2,1,0:T(8,128)} %heat_hbm.1) | copy-start | bytes 3145732
  1.9 1.2 %copy-start.1 = (f32[16,32,512]{2,1,0:T(8,128)S(1)}, f32[16,32,512]{2,1,0:T(8,128)}, u32[]{:S(2)}) copy-start(f32[16,32,512]{2,1,0:T(8,128)} %size_hbm.1) | copy-start | bytes 3145732
  3.1 1.2 %copy-start.2 = (f32[16,32,512]{2,1,0:T(8,128)S(1)}, f32[16,32,512]{2,1,0:T(8,128)}, u32[]{:S(2)}) copy-start(f32[16,32,512]{2,1,0:T(8,128)} %flux_hbm.1) | copy-start | bytes 3145732
  4.3 1.2 %copy-start.3 = (f32[16,32,512]{2,1,0:T(8,128)S(1)}, f32[16,32,512]{2,1,0:T(8,128)}, u32[]{:S(2)}) copy-start(f32[16,32,512]{2,1,0:T(8,128)} %goal_hbm.1) | copy-start | bytes 3145732
  5.5 1.2 %copy-start.4 = (f32[16,32,512]{2,1,0:T(8,128)S(1)}, f32[16,32,512]{2,1,0:T(8,128)}, u32[]{:S(2)}) copy-start(f32[16,32,512]{2,1,0:T(8,128)} %start_hbm.1) | copy-start | bytes 3145732

commit v2 on v1

--- a/solution.py
+++ b/solution.py
@@ -77,8 +77,16 @@
     peers = [lax.rem(seg + k, segments) for k in range(1, segments)]
     first = seg * rows
 
+    span = rows // 2
     loads = [
-        pltpu.make_async_copy(src, dst, in_sem.at[n])
+        [
+            pltpu.make_async_copy(
+                src.at[pl.ds(part_of * span, span)],
+                dst.at[pl.ds(part_of * span, span)],
+                in_sem.at[n, part_of],
+            )
+            for part_of in range(2)
+        ]
         for n, (src, dst) in enumerate(
             (
                 (start_hbm, state),
@@ -90,7 +98,12 @@
         )
     ]
     for load in loads:
-        load.start()
+        for copy in load:
+            copy.start()
+
+    def await_load(load):
+        for copy in load:
+            copy.wait()
 
     barrier = pltpu.get_barrier_semaphore()
     for peer in peers:
@@ -148,7 +161,7 @@
     def wide(line):
         return jnp.concatenate([line] * chunks, axis=1)
 
-    loads[0].wait()
+    await_load(loads[0])
 
     def pack(i, carry):
         halo_out[0, 0, pl.ds(i, 1), :] = state[i, width - 1 : width, :]
@@ -162,7 +175,7 @@
         copy.start()
 
     for load in loads[1:4]:
-        load.wait()
+        await_load(load)
 
     def pieces():
         for c in range(chunks):
@@ -238,7 +251,7 @@
         (jnp.zeros((width, axial), jnp.float32), jnp.ones((width, axial), jnp.float32)),
     )
 
-    loads[4].wait()
+    await_load(loads[4])
     sub = lax.broadcasted_iota(jnp.int32, (SUB, axial), 0)
     lane = lax.broadcasted_iota(jnp.int32, (SUB, axial), 1)
 
@@ -492,7 +505,7 @@
         return pl.pallas_call(
             functools.partial(kernel, segments, sectors),
             out_shape=(shape, shape),
-            in_specs=[pl.BlockSpec(memory_space=pl.ANY)] * 5,
+            in_specs=[pl.BlockSpec(memory_space=pltpu.HBM)] * 5,
             out_specs=[pl.BlockSpec(memory_space=pl.ANY)] * 2,
             scratch_shapes=[block] * 12
             + [
@@ -504,7 +517,7 @@
                 pltpu.VMEM((2, segments, 2) + tile, jnp.float32),
                 pltpu.VMEM((2, segments, 2) + tile, jnp.float32),
                 pltpu.VMEM((2, segments, 2) + tile, jnp.float32),
-                dma((5,)),
+                dma((5, 2)),
                 dma((2, 4)),
                 dma((2, 2)),
                 dma((2, 2)),

time: 39.7 us -> 39.8 us (level)
  no operation moved by 1% of the time
where the time goes in v2:
time: 39.8 us; the launch traced here: 39.5 us
  Pallas kernels  30.8 us (77%)
  local copies, waits for them, and re-layouts  8.06 us (20%)
  between operations  0.65 us (2%)
    pallas_call x1, Pallas kernels, body(): pl.pallas_call(functools.partial(kernel, segments, sectors), out_shape=(s...  30.8 us
    unnamed x12, local copies, waits for them, and re-layouts  8.06 us

profile of v2, /device:TPU:0, one launch (start us, length us, event | category | flops | bytes accessed | tf_op | source)
XLA Modules:
  0.0 39.5 jit_solution(2770525592893962573)
XLA Ops:
  0.6 0.0 copy-start
  0.6 1.2 %copy-done = f32[16,32,512]{2,1,0:T(8,128)S(1)} copy-done((f32[16,32,512]{2,1,0:T(8,128)S(1)}, f32[16,32,512]{2,1,0:T(8,128)}, u32[]{:S(2)}) %copy-start) | copy-done | bytes 1048600
  1.9 0.0 copy-start.1
  1.9 1.2 %copy-done.1 = f32[16,32,512]{2,1,0:T(8,128)S(1)} copy-done((f32[16,32,512]{2,1,0:T(8,128)S(1)}, f32[16,32,512]{2,1,0:T(8,128)}, u32[]{:S(2)}) %copy-start.1) | copy-done | bytes 1048600
  3.1 0.0 copy-start.2
  3.1 1.2 %copy-done.2 = f32[16,32,512]{2,1,0:T(8,128)S(1)} copy-done((f32[16,32,512]{2,1,0:T(8,128)S(1)}, f32[16,32,512]{2,1,0:T(8,128)}, u32[]{:S(2)}) %copy-start.2) | copy-done | bytes 1048600
  4.3 0.0 copy-start.3
  4.3 1.2 %copy-done.3 = f32[16,32,512]{2,1,0:T(8,128)S(1)} copy-done((f32[16,32,512]{2,1,0:T(8,128)S(1)}, f32[16,32,512]{2,1,0:T(8,128)}, u32[]{:S(2)}) %copy-start.3) | copy-done | bytes 1048600
  5.5 0.0 copy-start.4
  5.5 1.2 %copy-done.4 = f32[16,32,512]{2,1,0:T(8,128)S(1)} copy-done((f32[16,32,512]{2,1,0:T(8,128)S(1)}, f32[16,32,512]{2,1,0:T(8,128)}, u32[]{:S(2)}) %copy-start.4) | copy-done | bytes 1048600
  6.8 30.8 %shard_map.68 = (f32[16,32,512]{2,1,0:T(8,128)S(1)}, f32[16,32,512]{2,1,0:T(8,128)S(1)}) custom-call(f32[16,32,512]{2,1,0:T(8,128)S(1)} %copy-done, f32[16,32,512]{2,1,0:T(8,128)S(1)} %copy-done.1, f32[16,32,512]{2,1,0:T(8,128)S(1)} %copy-done.2, f32[16,32,512]{2,1,0:T(8,128)S(1)} %copy-done.3, f32[16,32,512]{2,1,0:T(8,128)S(1)} %copy-done.4), custom_call_target="tpu_custom_call" | custom-call | flops 31457280 | bytes 7340032 | tf_op jit(solution)/shard_map/pallas_call | solution.py:505
  37.5 1.0 %copy.9 = f32[16,32,512]{2,1,0:T(8,128)} copy(f32[16,32,512]{2,1,0:T(8,128)S(1)} %get-tuple-element.4) | data formatting | bytes 2097152
  38.5 1.0 %copy.10 = f32[16,32,512]{2,1,0:T(8,128)} copy(f32[16,32,512]{2,1,0:T(8,128)S(1)} %get-tuple-element.5) | data formatting | bytes 2097152
Async XLA Ops:
  0.6 1.2 %copy-start = (f32[16,32,512]{2,1,0:T(8,128)S(1)}, f32[16,32,512]{2,1,0:T(8,128)}, u32[]{:S(2)}) copy-start(f32[16,32,512]{2,1,0:T(8,128)} %heat_hbm.1) | copy-start | bytes 3145732
  1.9 1.2 %copy-start.1 = (f32[16,32,512]{2,1,0:T(8,128)S(1)}, f32[16,32,512]{2,1,0:T(8,128)}, u32[]{:S(2)}) copy-start(f32[16,32,512]{2,1,0:T(8,128)} %size_hbm.1) | copy-start | bytes 3145732
  3.1 1.2 %copy-start.2 = (f32[16,32,512]{2,1,0:T(8,128)S(1)}, f32[16,32,512]{2,1,0:T(8,128)}, u32[]{:S(2)}) copy-start(f32[16,32,512]{2,1,0:T(8,128)} %flux_hbm.1) | copy-start | bytes 3145732
  4.3 1.2 %copy-start.3 = (f32[16,32,512]{2,1,0:T(8,128)S(1)}, f32[16,32,512]{2,1,0:T(8,128)}, u32[]{:S(2)}) copy-start(f32[16,32,512]{2,1,0:T(8,128)} %goal_hbm.1) | copy-start | bytes 3145732
  5.5 1.2 %copy-start.4 = (f32[16,32,512]{2,1,0:T(8,128)S(1)}, f32[16,32,512]{2,1,0:T(8,128)}, u32[]{:S(2)}) copy-start(f32[16,32,512]{2,1,0:T(8,128)} %start_hbm.1) | copy-start | bytes 3145732

commit v3 on v2

--- a/solution.py
+++ b/solution.py
@@ -529,7 +529,7 @@
                 dma((2, segments)),
             ],
             compiler_params=pltpu.CompilerParams(
-                collective_id=0, has_side_effects=True, vmem_limit_bytes=32 * 2**20
+                collective_id=0, has_side_effects=True, vmem_limit_bytes=60 * 2**20
             ),
             cost_estimate=pl.CostEstimate(
                 flops=120 * cells, bytes_accessed=28 * cells, transcendentals=2 * cells

time: 39.8 us -> 35.6 us (0.89)
  local copies, waits for them, and re-layouts: 8.06 us -> 3.35 us
  Pallas kernels: 30.8 us -> 31.5 us
    unnamed x12 -> x4, local copies, waits for them, and re-layouts: 8.06 us -> 3.35 us
    pallas_call x1, Pallas kernels: 30.8 us -> 31.5 us  [body(): pl.pallas_call(functools.partial(kernel, segments, sectors), out_shape=(s...]
where the time goes in v3:
time: 35.6 us; the launch traced here: 35.4 us
  Pallas kernels  31.5 us (88%)
  local copies, waits for them, and re-layouts  3.35 us (9%)
  between operations  0.65 us (2%)
    pallas_call x1, Pallas kernels, body(): pl.pallas_call(functools.partial(kernel, segments, sectors), out_shape=(s...  31.5 us
    unnamed x4, local copies, waits for them, and re-layouts  3.35 us

profile of v3, /device:TPU:0, one launch (start us, length us, event | category | flops | bytes accessed | tf_op | source)
XLA Modules:
  0.0 35.4 jit_solution(17775580837930681241)
XLA Ops:
  0.6 31.5 %shard_map.68 = (f32[16,32,512]{2,1,0:T(8,128)}, f32[16,32,512]{2,1,0:T(8,128)}) custom-call(f32[16,32,512]{2,1,0:T(8,128)} %heat_hbm.1, f32[16,32,512]{2,1,0:T(8,128)} %size_hbm.1, f32[16,32,512]{2,1,0:T(8,128)} %flux_hbm.1, f32[16,32,512]{2,1,0:T(8,128)} %goal_hbm.1, f32[16,32,512]{2,1,0:T(8,128)} %start_hbm.1), custom_call_target="tpu_custom_call" | custom-call | flops 31457280 | bytes 7340032 | tf_op jit(solution)/shard_map/pallas_call | solution.py:505
  32.1 0.0 copy-start
  32.1 2.4 %copy.9 = f32[16,32,512]{2,1,0:T(8,128)} copy(f32[16,32,512]{2,1,0:T(8,128)} %get-tuple-element.4) | data formatting | bytes 2097152
  34.5 0.0 copy-done
  34.5 1.0 %copy.10 = f32[16,32,512]{2,1,0:T(8,128)} copy(f32[16,32,512]{2,1,0:T(8,128)S(1)} %copy-done) | data formatting | bytes 2097152
Async XLA Ops:
  32.1 2.4 %copy-start = (f32[16,32,512]{2,1,0:T(8,128)S(1)}, f32[16,32,512]{2,1,0:T(8,128)}, u32[]{:S(2)}) copy-start(f32[16,32,512]{2,1,0:T(8,128)} %get-tuple-element.5) | copy-start | bytes 3145732

commit v4 on v3

--- a/solution.py
+++ b/solution.py
@@ -222,7 +222,7 @@
         one = jnp.ones((width, half), jnp.float32)
         zero = jnp.zeros((width, half), jnp.float32)
         _, ea, _, va, upper = lax.fori_loop(
-            0, rows, eliminate, (one, one, one, zero, zero)
+            0, rows, eliminate, (one, one, one, zero, zero), unroll=4
         )
         scatter(coef_out, 0, va, 2 * h, 2 * h + 2)
         scatter(coef_out, 1, ea, 2 * h, 2 * h + 2)
@@ -249,6 +249,7 @@
         rows,
         respond,
         (jnp.zeros((width, axial), jnp.float32), jnp.ones((width, axial), jnp.float32)),
+        unroll=4,
     )
 
     await_load(loads[4])
@@ -302,7 +303,7 @@
             return tuple(new)
 
         zero = jnp.zeros((SUB, axial), jnp.float32)
-        sums = lax.fori_loop(0, rows, step, tuple((zero, zero) for _ in chosen))
+        sums = lax.fori_loop(0, rows, step, tuple((zero, zero) for _ in chosen), unroll=2)
         for g, pair in zip(chosen, sums):
             for slot, plane in enumerate(pair):
                 for owner, where_rows, c in pieces():
@@ -339,8 +340,8 @@
             return p
 
         zero = jnp.zeros((width, axial), jnp.float32)
-        lax.fori_loop(0, rows, forward, zero)
-        lax.fori_loop(0, rows, backward, zero)
+        lax.fori_loop(0, rows, forward, zero, unroll=4)
+        lax.fori_loop(0, rows, backward, zero, unroll=4)
 
     def reduced_factors():
         factors, beta = [], None
@@ -434,7 +435,7 @@
         heat[i] = slope_weight * rise - size[i]
         return carry
 
-    lax.fori_loop(0, rows, slope, 0)
+    lax.fori_loop(0, rows, slope, 0, unroll=4)
 
     await_back(0)
     a, b = ends(0)
@@ -446,7 +447,7 @@
         halo_out[1, 1, pl.ds(i, 1), :] = x[0:1, :]
         return carry
 
-    lax.fori_loop(0, rows, advance, 0)
+    lax.fori_loop(0, rows, advance, 0, unroll=4)
     halos = halo_copies(1)
     for copy in halos:
         copy.start()
@@ -472,7 +473,7 @@
             out_s[i] = x * heat[i]
             return carry
 
-        lax.fori_loop(n * quarter, (n + 1) * quarter, finish, 0)
+        lax.fori_loop(n * quarter, (n + 1) * quarter, finish, 0, unroll=4)
         span = slice(n * quarter, (n + 1) * quarter)
         for m, (src, dst) in enumerate(((out_x, adjoint_hbm), (out_s, sens_hbm))):
             store = pltpu.make_async_copy(

time: 35.6 us -> 34.2 us (0.961)
  Pallas kernels: 31.5 us -> 30.1 us
    pallas_call x1, Pallas kernels: 31.5 us -> 30.1 us  [body(): pl.pallas_call(functools.partial(kernel, segments, sectors), out_shape=(s...]
where the time goes in v4:
time: 34.2 us; the launch traced here: 34.1 us
  Pallas kernels  30.1 us (88%)
  local copies, waits for them, and re-layouts  3.35 us (10%)
  between operations  0.65 us (2%)
    pallas_call x1, Pallas kernels, body(): pl.pallas_call(functools.partial(kernel, segments, sectors), out_shape=(s...  30.1 us
    unnamed x4, local copies, waits for them, and re-layouts  3.35 us

profile of v4, /device:TPU:0, one launch (start us, length us, event | category | flops | bytes accessed | tf_op | source)
XLA Modules:
  0.0 34.1 jit_solution(12797611623418956310)
XLA Ops:
  0.6 30.1 %shard_map.68 = (f32[16,32,512]{2,1,0:T(8,128)}, f32[16,32,512]{2,1,0:T(8,128)}) custom-call(f32[16,32,512]{2,1,0:T(8,128)} %heat_hbm.1, f32[16,32,512]{2,1,0:T(8,128)} %size_hbm.1, f32[16,32,512]{2,1,0:T(8,128)} %flux_hbm.1, f32[16,32,512]{2,1,0:T(8,128)} %goal_hbm.1, f32[16,32,512]{2,1,0:T(8,128)} %start_hbm.1), custom_call_target="tpu_custom_call" | custom-call | flops 31457280 | bytes 7340032 | tf_op jit(solution)/shard_map/pallas_call | solution.py:506
  30.7 0.0 copy-start
  30.7 2.4 %copy.9 = f32[16,32,512]{2,1,0:T(8,128)} copy(f32[16,32,512]{2,1,0:T(8,128)} %get-tuple-element.4) | data formatting | bytes 2097152
  33.1 0.0 copy-done
  33.1 1.0 %copy.10 = f32[16,32,512]{2,1,0:T(8,128)} copy(f32[16,32,512]{2,1,0:T(8,128)S(1)} %copy-done) | data formatting | bytes 2097152
Async XLA Ops:
  30.7 2.4 %copy-start = (f32[16,32,512]{2,1,0:T(8,128)S(1)}, f32[16,32,512]{2,1,0:T(8,128)}, u32[]{:S(2)}) copy-start(f32[16,32,512]{2,1,0:T(8,128)} %get-tuple-element.5) | copy-start | bytes 3145732

commit v5 on v4

--- a/solution.py
+++ b/solution.py
@@ -51,6 +51,9 @@
     u_in,
     ret_out,
     ret_in,
+    factor,
+    side_a,
+    side_b,
     in_sem,
     out_sem,
     halo_ssem,
@@ -66,7 +69,9 @@
     groups = width // SUB
     chunks = axial // LANES
     per_chunk = segments // chunks
-    tile_rows = width // per_chunk
+    tile_rows = width // (2 * per_chunk)
+    inner, outer = tuple(range(1, groups - 1)), (0, groups - 1)
+    halves = (inner, outer)
     total = rows * segments
     stiffness = radial_weight * rows * rows
 
@@ -177,16 +182,23 @@
     for load in loads[1:4]:
         await_load(load)
 
+    def rows_of(g):
+        return slice(g * SUB, (g + 1) * SUB)
+
     def pieces():
         for c in range(chunks):
             for k in range(per_chunk):
-                yield c * per_chunk + k, slice(k * tile_rows, (k + 1) * tile_rows), c
-
-    def scatter(ref, slot, plane, c_first, c_last):
-        for owner, where_rows, c in pieces():
-            if c_first <= c < c_last:
-                at = (c - c_first) * LANES
-                ref[owner, slot] = plane[where_rows, at : at + LANES]
+                where_rows = slice(k * tile_rows, (k + 1) * tile_rows)
+                where_cols = slice(c * LANES, (c + 1) * LANES)
+                yield c * per_chunk + k, where_rows, where_cols
+
+    def scatter(slot, plane, c_first, c_last):
+        for n, chosen in enumerate(halves):
+            lines = jnp.concatenate([plane[rows_of(g)] for g in chosen], axis=0)
+            for owner, where_rows, cols in pieces():
+                if c_first * LANES <= cols.start < c_last * LANES:
+                    at = cols.start - c_first * LANES
+                    coef_out[owner, slot, n] = lines[where_rows, at : at + LANES]
 
     half = 2 * LANES
     for h in range(axial // half):
@@ -224,9 +236,9 @@
         _, ea, _, va, upper = lax.fori_loop(
             0, rows, eliminate, (one, one, one, zero, zero), unroll=4
         )
-        scatter(coef_out, 0, va, 2 * h, 2 * h + 2)
-        scatter(coef_out, 1, ea, 2 * h, 2 * h + 2)
-        scatter(coef_out, 2, upper, 2 * h, 2 * h + 2)
+        scatter(0, va, 2 * h, 2 * h + 2)
+        scatter(1, ea, 2 * h, 2 * h + 2)
+        scatter(2, upper, 2 * h, 2 * h + 2)
 
     coef_sends = sends(coef_out, coef_in, coef_ssem, coef_rsem)
     for copy in coef_sends:
@@ -256,7 +268,9 @@
     sub = lax.broadcasted_iota(jnp.int32, (SUB, axial), 0)
     lane = lax.broadcasted_iota(jnp.int32, (SUB, axial), 1)
 
-    def right_side(sweep, chosen):
+    def right_side(sweep, half):
+        chosen = halves[half]
+
         def step(i, carry):
             radius, _, _ = geometry(i)
             az = wide(azimuth_coef(radius))
@@ -304,128 +318,129 @@
 
         zero = jnp.zeros((SUB, axial), jnp.float32)
         sums = lax.fori_loop(0, rows, step, tuple((zero, zero) for _ in chosen), unroll=2)
-        for g, pair in zip(chosen, sums):
-            for slot, plane in enumerate(pair):
-                for owner, where_rows, c in pieces():
-                    at = g * SUB - where_rows.start
-                    if 0 <= at < tile_rows:
-                        u_out[sweep, owner, slot, at : at + SUB, :] = plane[
-                            :, c * LANES : (c + 1) * LANES
-                        ]
-
-    def send_ends(sweep):
-        copies = sends(
-            u_out.at[sweep], u_in.at[sweep], u_ssem.at[sweep], u_rsem.at[sweep]
-        )
+        for slot in range(2):
+            lines = jnp.concatenate([pair[slot] for pair in sums], axis=0)
+            for owner, where_rows, cols in pieces():
+                u_out[sweep, half, owner, slot] = lines[where_rows, cols]
+
+    def send_ends(sweep, half):
+        at = (sweep, half)
+        copies = sends(u_out.at[at], u_in.at[at], u_ssem.at[at], u_rsem.at[at])
         for copy in copies:
             copy.start()
-        u_in[sweep, seg] = u_out[sweep, seg]
+        u_in[sweep, half, seg] = u_out[sweep, half, seg]
         return copies
 
-    def await_ends(sweep):
-        await_from(u_out.at[sweep], u_in.at[sweep], u_ssem.at[sweep], u_rsem.at[sweep])
-
-    def substitute():
-        def forward(i, g):
+    def await_ends(sweep, half):
+        at = (sweep, half)
+        await_from(u_out.at[at], u_in.at[at], u_ssem.at[at], u_rsem.at[at])
+
+    def substitute(half):
+        chosen = halves[half]
+
+        def forward(i, carry):
             _, low, _ = geometry(i)
-            g = inv[i] * (rhs[i] + low * g)
-            rhs[i] = g
-            return g
-
-        def backward(n, p):
+            new = []
+            for g, before in zip(chosen, carry):
+                here = rows_of(g)
+                now = inv[i, here, :] * (rhs[i, here, :] + low * before)
+                rhs[i, here, :] = now
+                new.append(now)
+            return tuple(new)
+
+        def backward(n, carry):
             i = rows - 1 - n
             _, _, high = geometry(i)
-            p = rhs[i] + (high * inv[i]) * p
-            part[i] = p
-            return p
-
-        zero = jnp.zeros((width, axial), jnp.float32)
+            new = []
+            for g, after in zip(chosen, carry):
+                here = rows_of(g)
+                now = rhs[i, here, :] + (high * inv[i, here, :]) * after
+                part[i, here, :] = now
+                new.append(now)
+            return tuple(new)
+
+        zero = tuple(jnp.zeros((SUB, axial), jnp.float32) for _ in chosen)
         lax.fori_loop(0, rows, forward, zero, unroll=4)
         lax.fori_loop(0, rows, backward, zero, unroll=4)
 
-    def reduced_factors():
-        factors, beta = [], None
+    def reduced_factors(half):
+        beta = None
         for s in range(segments):
-            v_first, v_last, w_last = coef_in[s, 0], coef_in[s, 1], coef_in[s, 2]
+            v_first, v_last, w_last = [coef_in[s, slot, half] for slot in range(3)]
             w_first = v_last * ((segments + s + 1.0) / (segments + s))
             if s == 0:
-                factors.append((None, None, None, w_first, w_last, None))
                 beta = w_last
+                factor[half, s, 3] = beta
                 continue
             scale = 1.0 / (1.0 - v_first * beta)
             q = scale * w_first
             cross = v_last * beta
-            new_beta = w_last + cross * q
-            factors.append((scale, scale * v_first, v_last, q, new_beta, cross))
-            beta = new_beta
-        return factors
-
-    def reduced_solve(sweep, factors):
+            beta = w_last + cross * q
+            for slot, plane in enumerate((scale, scale * v_first, q, beta, cross)):
+                factor[half, s, slot] = plane
+
+    def reduced_solve(sweep, half):
         firsts, lasts = [], []
         for s in range(segments):
-            u_first = u_in[sweep, s, 0] * (segments / (stiffness * (segments + s)))
-            u_last = u_in[sweep, s, 1] * (segments / (stiffness * (segments + s + 1)))
+            end = [u_in[sweep, half, s, slot] for slot in range(2)]
+            u_first = end[0] * (segments / (stiffness * (segments + s)))
+            u_last = end[1] * (segments / (stiffness * (segments + s + 1)))
             if s == 0:
                 firsts.append(u_first)
                 lasts.append(u_last)
                 continue
-            scale, scaled_v, v_last, _, _, cross = factors[s]
-            p = scale * u_first + scaled_v * lasts[s - 1]
+            p = factor[half, s, 0] * u_first + factor[half, s, 1] * lasts[s - 1]
             firsts.append(p)
-            lasts.append(u_last + v_last * lasts[s - 1] + cross * p)
-        blank = jnp.zeros((tile_rows, LANES), jnp.float32)
-        beyond = blank
-        ret_out[sweep, 0, 0] = blank
+            lasts.append(
+                u_last + coef_in[s, 1, half] * lasts[s - 1] + factor[half, s, 4] * p
+            )
+        beyond = jnp.zeros((tile_rows, LANES), jnp.float32)
+        ret_out[sweep, half, 0, 0] = beyond
         for s in range(segments - 1, -1, -1):
-            ret_out[sweep, s, 1] = beyond
+            ret_out[sweep, half, s, 1] = beyond
             if s < segments - 1:
-                ret_out[sweep, s + 1, 0] = lasts[s] + factors[s][4] * beyond
-            beyond = firsts[s] + factors[s][3] * beyond if s > 0 else beyond
-
-    def send_back(sweep):
-        copies = sends(
-            ret_out.at[sweep], ret_in.at[sweep], ret_ssem.at[sweep], ret_rsem.at[sweep]
-        )
+                ret_out[sweep, half, s + 1, 0] = lasts[s] + factor[half, s, 3] * beyond
+            if s > 0:
+                beyond = firsts[s] + factor[half, s, 2] * beyond
+
+    def send_back(sweep, half):
+        at = (sweep, half)
+        copies = sends(ret_out.at[at], ret_in.at[at], ret_ssem.at[at], ret_rsem.at[at])
         for copy in copies:
             copy.start()
-        ret_in[sweep, seg] = ret_out[sweep, seg]
+        ret_in[sweep, half, seg] = ret_out[sweep, half, seg]
         return copies
 
-    def await_back(sweep):
-        await_from(
-            ret_out.at[sweep], ret_in.at[sweep], ret_ssem.at[sweep], ret_rsem.at[sweep]
-        )
-
-    def ends(sweep):
-        planes = []
-        for slot in range(2):
-            planes.append(
-                jnp.concatenate(
-                    [
-                        jnp.concatenate(
-                            [
-                                ret_in[sweep, c * per_chunk + k, slot]
-                                for k in range(per_chunk)
-                            ],
-                            axis=0,
-                        )
-                        for c in range(chunks)
-                    ],
-                    axis=1,
-                )
-            )
-        return planes
+    def ends(sweep, half):
+        at = (sweep, half)
+        await_from(ret_out.at[at], ret_in.at[at], ret_ssem.at[at], ret_rsem.at[at])
+        for owner, where_rows, cols in pieces():
+            side_a[half, where_rows, cols] = ret_in[sweep, half, owner, 0]
+            side_b[half, where_rows, cols] = ret_in[sweep, half, owner, 1]
+        return [
+            (side_a[half, rows_of(n), :], side_b[half, rows_of(n), :])
+            for n in range(len(halves[half]))
+        ]
+
+    def solved(i, half, sides):
+        for g, (a, b) in zip(halves[half], sides):
+            here = rows_of(g)
+            yield g, part[i, here, :] + qa[i, here, :] * a + rb[i, here, :] * b
 
     for copy in halos:
         copy.wait_recv()
-    right_side(0, tuple(range(groups)))
-    started = [coef_sends, halos, send_ends(0)]
-    substitute()
+    started = [coef_sends, halos]
+    for half in (1, 0):
+        right_side(0, half)
+        started.append(send_ends(0, half))
     await_from(coef_out, coef_in, coef_ssem, coef_rsem)
-    factors = reduced_factors()
-    await_ends(0)
-    reduced_solve(0, factors)
-    started.append(send_back(0))
+    for half in (1, 0):
+        reduced_factors(half)
+    for half in (1, 0):
+        substitute(half)
+        await_ends(0, half)
+        reduced_solve(0, half)
+        started.append(send_back(0, half))
 
     last_lane = lax.broadcasted_iota(jnp.int32, (width, axial), 1) == axial - 1
 
@@ -437,52 +452,57 @@
 
     lax.fori_loop(0, rows, slope, 0, unroll=4)
 
-    await_back(0)
-    a, b = ends(0)
-
-    def advance(i, carry):
-        x = part[i] + qa[i] * a + rb[i] * b
-        state[i] = x
-        halo_out[1, 0, pl.ds(i, 1), :] = x[width - 1 : width, :]
-        halo_out[1, 1, pl.ds(i, 1), :] = x[0:1, :]
-        return carry
-
-    lax.fori_loop(0, rows, advance, 0, unroll=4)
-    halos = halo_copies(1)
-    for copy in halos:
-        copy.start()
-
-    for copy in halos:
-        copy.wait_recv()
-    right_side(1, tuple(range(groups)))
-    started += [halos, send_ends(1)]
-    substitute()
-    await_ends(1)
-    reduced_solve(1, reduced_factors())
-    started.append(send_back(1))
-    await_back(1)
-    a, b = ends(1)
-
-    quarter = rows // 4
+    for half in (1, 0):
+        sides = ends(0, half)
+
+        def advance(i, carry):
+            for g, x in solved(i, half, sides):
+                state[i, rows_of(g), :] = x
+                if g == groups - 1:
+                    halo_out[1, 0, pl.ds(i, 1), :] = x[SUB - 1 : SUB, :]
+                if g == 0:
+                    halo_out[1, 1, pl.ds(i, 1), :] = x[0:1, :]
+            return carry
+
+        lax.fori_loop(0, rows, advance, 0, unroll=4)
+        if half == 1:
+            halos = halo_copies(1)
+            started.append(halos)
+            for copy in halos:
+                copy.start()
+
+    for half in (0, 1):
+        if half == 1:
+            for copy in halos:
+                copy.wait_recv()
+        right_side(1, half)
+        started.append(send_ends(1, half))
+    for half in (0, 1):
+        substitute(half)
+        await_ends(1, half)
+        reduced_solve(1, half)
+        started.append(send_back(1, half))
+
     stores = []
-    for n in range(4):
+    for half in (0, 1):
+        sides = ends(1, half)
 
         def finish(i, carry):
-            x = part[i] + qa[i] * a + rb[i] * b
-            out_x[i] = x
-            out_s[i] = x * heat[i]
+            for g, x in solved(i, half, sides):
+                here = rows_of(g)
+                out_x[i, here, :] = x
+                out_s[i, here, :] = x * heat[i, here, :]
             return carry
 
-        lax.fori_loop(n * quarter, (n + 1) * quarter, finish, 0, unroll=4)
-        span = slice(n * quarter, (n + 1) * quarter)
-        for m, (src, dst) in enumerate(((out_x, adjoint_hbm), (out_s, sens_hbm))):
-            store = pltpu.make_async_copy(
-                src.at[pl.ds(n * quarter, quarter)],
-                dst.at[pl.ds(n * quarter, quarter)],
-                out_sem.at[m, n],
-            )
-            store.start()
-            stores.append(store)
+        lax.fori_loop(0, rows, finish, 0, unroll=4)
+        for g in halves[half]:
+            here = pl.ds(g * SUB, SUB)
+            for m, (src, dst) in enumerate(((out_x, adjoint_hbm), (out_s, sens_hbm))):
+                store = pltpu.make_async_copy(
+                    src.at[:, here], dst.at[:, here], out_sem.at[m, g]
+                )
+                store.start()
+                stores.append(store)
 
     for copies in started:
         for copy in copies:
@@ -497,7 +517,8 @@
 
     def body(heat, size, flux, goal, start):
         rows, width, axial = heat.shape
-        tile_rows = width * axial // (segments * LANES)
+        half_rows = width // 2
+        tile_rows = half_rows * axial // (segments * LANES)
         block = pltpu.VMEM((rows, width, axial), jnp.float32)
         tile = (tile_rows, LANES)
         shape = jax.ShapeDtypeStruct((rows, width, axial), jnp.float32)
@@ -512,22 +533,25 @@
             + [
                 pltpu.VMEM((2, 2, rows, axial), jnp.float32),
                 pltpu.VMEM((2, 2, rows, axial), jnp.float32),
-                pltpu.VMEM((segments, 3) + tile, jnp.float32),
-                pltpu.VMEM((segments, 3) + tile, jnp.float32),
-                pltpu.VMEM((2, segments, 2) + tile, jnp.float32),
-                pltpu.VMEM((2, segments, 2) + tile, jnp.float32),
-                pltpu.VMEM((2, segments, 2) + tile, jnp.float32),
-                pltpu.VMEM((2, segments, 2) + tile, jnp.float32),
+                pltpu.VMEM((segments, 3, 2) + tile, jnp.float32),
+                pltpu.VMEM((segments, 3, 2) + tile, jnp.float32),
+                pltpu.VMEM((2, 2, segments, 2) + tile, jnp.float32),
+                pltpu.VMEM((2, 2, segments, 2) + tile, jnp.float32),
+                pltpu.VMEM((2, 2, segments, 2) + tile, jnp.float32),
+                pltpu.VMEM((2, 2, segments, 2) + tile, jnp.float32),
+                pltpu.VMEM((2, segments, 5) + tile, jnp.float32),
+                pltpu.VMEM((2, half_rows, axial), jnp.float32),
+                pltpu.VMEM((2, half_rows, axial), jnp.float32),
                 dma((5, 2)),
-                dma((2, 4)),
+                dma((2, width // SUB)),
                 dma((2, 2)),
                 dma((2, 2)),
                 dma((segments,)),
                 dma((segments,)),
-                dma((2, segments)),
-                dma((2, segments)),
-                dma((2, segments)),
-                dma((2, segments)),
+                dma((2, 2, segments)),
+                dma((2, 2, segments)),
+                dma((2, 2, segments)),
+                dma((2, 2, segments)),
             ],
             compiler_params=pltpu.CompilerParams(
                 collective_id=0, has_side_effects=True, vmem_limit_bytes=60 * 2**20

time: 34.2 us -> 31.6 us (0.924)
  Pallas kernels: 30.1 us -> 27.5 us
    pallas_call x1, Pallas kernels: 30.1 us -> 27.5 us  [body(): pl.pallas_call(functools.partial(kernel, segments, sectors), out_shape=(s...]
where the time goes in v5:
time: 31.6 us; the launch traced here: 31.4 us
  Pallas kernels  27.5 us (87%)
  local copies, waits for them, and re-layouts  3.35 us (11%)
  between operations  0.65 us (2%)
    pallas_call x1, Pallas kernels, body(): pl.pallas_call(functools.partial(kernel, segments, sectors), out_shape=(s...  27.5 us
    unnamed x4, local copies, waits for them, and re-layouts  3.35 us

profile of v5, /device:TPU:0, one launch (start us, length us, event | category | flops | bytes accessed | tf_op | source)
XLA Modules:
  0.0 31.4 jit_solution(8880992448274264291)
XLA Ops:
  0.6 27.5 %shard_map.68 = (f32[16,32,512]{2,1,0:T(8,128)}, f32[16,32,512]{2,1,0:T(8,128)}) custom-call(f32[16,32,512]{2,1,0:T(8,128)} %heat_hbm.1, f32[16,32,512]{2,1,0:T(8,128)} %size_hbm.1, f32[16,32,512]{2,1,0:T(8,128)} %flux_hbm.1, f32[16,32,512]{2,1,0:T(8,128)} %goal_hbm.1, f32[16,32,512]{2,1,0:T(8,128)} %start_hbm.1), custom_call_target="tpu_custom_call" | custom-call | flops 31457280 | bytes 7340032 | tf_op jit(solution)/shard_map/pallas_call | solution.py:527
  28.1 0.0 copy-start
  28.1 2.4 %copy.9 = f32[16,32,512]{2,1,0:T(8,128)} copy(f32[16,32,512]{2,1,0:T(8,128)} %get-tuple-element.4) | data formatting | bytes 2097152
  30.5 0.0 copy-done
  30.5 1.0 %copy.10 = f32[16,32,512]{2,1,0:T(8,128)} copy(f32[16,32,512]{2,1,0:T(8,128)S(1)} %copy-done) | data formatting | bytes 2097152
Async XLA Ops:
  28.1 2.4 %copy-start = (f32[16,32,512]{2,1,0:T(8,128)S(1)}, f32[16,32,512]{2,1,0:T(8,128)}, u32[]{:S(2)}) copy-start(f32[16,32,512]{2,1,0:T(8,128)} %get-tuple-element.5) | copy-start | bytes 3145732
